TPU v7x, 1024 devices: a whole 4x4x32 slice. The times are simulated.
1024 devices in a mesh: expert: 16 (over z_lo, core), replica: 16 (over y, x), micro: 4 (over z_hi).
Axes of the slice: x: 4, y: 4, z: 32 (z_hi: 4, z_lo: 8; z = z_hi * 8 + z_lo), core: 2. Of those that a mesh axis runs over, the one named last changes fastest.
Arguments:
- grad_rows: bfloat16 [131072, 3584], P(('expert', 'replica', 'micro')), may hold values from -0.19921875 to 0.19921875
- routing: int32 [131072, 1], P(('expert', 'replica', 'micro')), may hold values from 0 to 15; in each aligned block of 128 rows (0 to 127, 128 to 255, ...) at most 10 rows name the same one
- route_weight: float32 [131072, 1], P(('expert', 'replica', 'micro')), may hold values from 0.05 to 1
- saved_hidden: bfloat16 [163840, 1024], P(('expert', 'replica', 'micro')), may hold values from -24 to 24
Outputs:
- grad_weight: float32 [16, 1024, 3584], P('expert', 'replica', 'micro')
Inputs may be any that keep to these rules, and one draw needn't show every extreme that they name: `routing`: the tokens of one device name one expert in at most 10 rows; in every draw some device names some expert in exactly 10 rows.
All inputs are finite; a program needn't handle non-finite values.
Results may differ from a plain program's by a relative error of at most 0.015.
Values may be sent and summed in bfloat16 or wider, within the bound.
No kernel may reach another device: no remote copies, remote signals or barrier semaphores. Data moves between devices by JAX's collectives and lax.ppermute only.
A program may use at most 64 MiB of HBM per device.

v0:
```python
import jax
import jax.numpy as jnp
from jax import lax
from jax.sharding import PartitionSpec as P


def shards(grad_rows, routing, route_weight, saved_hidden):
    expert_count = lax.axis_size("expert")
    slot_count = saved_hidden.shape[0]
    capacity = slot_count // expert_count
    row_width = grad_rows.shape[1]
    targets = routing[:, 0]
    member = (targets[:, None] == jnp.arange(expert_count, dtype=jnp.int32)[None, :]).astype(
        jnp.int32
    )
    position = jnp.sum(member * (jnp.cumsum(member, axis=0) - 1), axis=1)
    slot_index = targets * capacity + position
    placing = (jnp.arange(slot_count, dtype=jnp.int32)[:, None] == slot_index[None, :]).astype(
        jnp.bfloat16
    )
    scaled = (grad_rows.astype(jnp.float32) * route_weight).astype(jnp.bfloat16)
    outgoing = jnp.dot(placing, scaled, preferred_element_type=jnp.float32).astype(jnp.bfloat16)
    outgoing = outgoing.reshape(expert_count, capacity, row_width)
    arrived = lax.all_to_all(outgoing, "expert", split_axis=0, concat_axis=0, tiled=True)
    quarters = lax.all_to_all(
        arrived.reshape(slot_count, row_width), "micro", split_axis=1, concat_axis=0, tiled=True
    )
    hidden = lax.all_gather(saved_hidden, "micro", axis=0, tiled=True)
    summed = lax.psum_scatter(
        lax.dot_general(
            hidden, quarters, (((0,), (0,)), ((), ())), preferred_element_type=jnp.float32
        ).astype(jnp.bfloat16),
        "replica",
        scatter_dimension=0,
        tiled=True,
    ).astype(jnp.float32)
    return summed[None]


def solution(mesh):
    return jax.shard_map(
        shards,
        mesh=mesh,
        in_specs=(
            P(("expert", "replica", "micro"), None),
            P(("expert", "replica", "micro"), None),
            P(("expert", "replica", "micro"), None),
            P(("expert", "replica", "micro"), None),
        ),
        out_specs=P("expert", "replica", "micro"),
        check_vma=False,
    )
```

profile of v0, /device:TPU:2, one launch (start us, length us, event | category | flops | bytes accessed | tf_op | source)
XLA Modules:
  0.0 444.9 jit_solution(658669605400340606)
XLA Ops:
  6.5 0.7 fusion.1
  7.3 0.2 reduce_window_sum.11
  7.4 0.8 select_reduce_fusion
  8.3 0.7 multiply_add_fusion
  8.9 1.7 convolution_convert_fusion
  10.7 0.4 reshape.16
  11.1 96.7 %all_to_all.24 = bf16[16,10,3584]{2,1,0:T(8,128)(2,1)} all-to-all(bf16[16,10,3584]{2,1,0:T(8,128)(2,1)S(1)} %reshape.16), channel_id=1, replica_groups=mesh['expert'=16,'replica'=16,'micro'=4] {'expert'}, dimensions={0} | all-to-all | bytes 2293760 | tf_op jit(solution)/shard_map/all_to_all | solution.py:24
  107.8 2.9 all_to_all.18
  110.8 1.1 copy.8
  111.9 20.8 %all-to-all-start.1 = ((bf16[160,4,896]{2,0,1:T(8,128)(2,1)}), bf16[160,4,896]{2,0,1:T(8,128)(2,1)S(1)}, u32[]{:S(2)}, u32[]{:S(2)}) async-start(bf16[160,4,896]{2,0,1:T(8,128)(2,1)} %copy.8), calls=%async_computation.1 | async-start | bytes 2293760 | tf_op jit(solution)/shard_map/all_to_all | solution.py:25
  132.7 0.0 all-gather.2.cloned.1.call-start
  132.7 0.7 all-gather.2.cloned.1.call-update
  133.5 0.0 reduce-scatter.4.cloned.1.call-start
  133.5 197.8 %all-gather.2.cloned.1.call-done = bf16[640,1024]{1,0:T(8,128)(2,1)} async-done(((bf16[160,1024]{1,0:T(8,128)(2,1)}), bf16[640,1024]{1,0:T(8,128)(2,1)}) %all-gather.2.cloned.1.call-update) | async-done | bytes 1310736 | tf_op jit(solution)/shard_map/all_gather | solution.py:28
  331.3 0.0 all-to-all-done.1
  331.3 2.9 convert_bitcast_fusion
  334.3 2.5 copy.10
  336.8 0.0 reduce-scatter.4.cloned.1.call-update
  336.8 99.3 %reduce-scatter.4.cloned.1.call-done = bf16[64,896]{1,0:T(8,128)(2,1)} async-done(((bf16[1024,896]{1,0:T(8,128)(2,1)}), bf16[64,896]{1,0:T(8,128)(2,1)}) %reduce-scatter.4.cloned.1.call-update) | async-done | bytes 114704
  436.1 1.1 copy.11
  437.2 0.9 copy.9
  (1 shorter events, 0.0 us)
Async XLA Ops:
  111.9 219.4 %all-to-all-start.1 = ((bf16[160,4,896]{2,0,1:T(8,128)(2,1)}), bf16[160,4,896]{2,0,1:T(8,128)(2,1)S(1)}, u32[]{:S(2)}, u32[]{:S(2)}) async-start(bf16[160,4,896]{2,0,1:T(8,128)(2,1)} %copy.8), calls=%async_computation.1 | async-start | bytes 2293760 | tf_op jit(solution)/shard_map/all_to_all | solution.py:25
  132.7 198.6 %all-gather.2.cloned.1.call-start = ((), (), s32[]{:S(2)}) async-start(), calls=%async_computation.3 | async-start | bytes 1638400 | tf_op jit(solution)/shard_map/all_gather | solution.py:28
  133.5 302.6 %reduce-scatter.4.cloned.1.call-start = ((), (), s32[]{:S(2)}) async-start(), calls=%async_computation.4 | async-start | bytes 1949696
Sparse Core Ops, SparseCore 0:
  136.2 195.0 all-gather.1
  336.9 99.0 reduce-scatter.3
where the time goes:
time: 445 us
  waiting for transfers between devices  298 us (67%)
  blocking collectives  96.7 us (22%)
  starting transfers between devices  20.9 us (5%)
  between operations  13.5 us (3%)
  local copies, waits for them, and re-layouts  8.93 us (2%)
  matrix products  4.66 us (1%)
    all_gather x1, waiting for transfers between devices, shards(): hidden = lax.all_gather(saved_hidden, 'micro', axis=0, tiled=True)  198 us
    unnamed x3, waiting for transfers between devices  100 us
    all_to_all x1, blocking collectives, shards(): lax.all_to_all(outgoing, 'expert', split_axis=0, concat_axis=0, tiled=True)  96.7 us
    all_to_all x1, starting transfers between devices, shards(): lax.all_to_all(arrived.reshape(slot_count, row_width), 'micro', split_axi...  20.8 us
  transfers between devices with their start and end apart: 3, of which 2 were waited for; matrix products, arithmetic and copies ran while one was open for 0% of the time, Pallas kernels for 0%

commit v1 on v0

v1 whole, which is shorter than its diff:
```python
import functools

import jax
import jax.numpy as jnp
from jax import lax
from jax.experimental import pallas as pl
from jax.experimental.pallas import tpu as pltpu
from jax.sharding import PartitionSpec as P

FIRST = 8
VMEM = 48 * 1024 * 1024


def iota(shape, dimension):
    return lax.broadcasted_iota(jnp.int32, shape, dimension)


def dispatch_kernel(capacity, parts, rows_ref, target_ref, weight_ref, out_ref):
    tokens, width = rows_ref.shape
    experts = out_ref.shape[0] // FIRST
    part = width // parts
    extra = capacity - FIRST
    target, weight = target_ref[...], weight_ref[...]
    member = iota((experts, tokens), 0) == target
    earlier = (iota((tokens, tokens), 0) < iota((tokens, tokens), 1)).astype(jnp.bfloat16)
    before = jnp.dot(member.astype(jnp.bfloat16), earlier, preferred_element_type=jnp.float32)
    position = jnp.sum(jnp.where(member, before, 0.0), axis=0, keepdims=True).astype(jnp.int32)
    row = iota((experts * FIRST, tokens), 0)
    expert, local = row // FIRST, row % FIRST
    mine = expert == target
    first = mine & (local == position)
    first_weight = jnp.sum(jnp.where(first, weight, 0.0), axis=1, keepdims=True)
    first = first.astype(jnp.bfloat16)
    for start in range(0, width, part):
        piece = jnp.dot(first, rows_ref[:, start : start + part], preferred_element_type=jnp.float32)
        out_ref[:, start : start + part] = (piece * first_weight).astype(jnp.bfloat16)
    late = mine & (FIRST + local % extra == position)
    late_weight = jnp.sum(jnp.where(late, weight, 0.0), axis=1, keepdims=True)
    total = jnp.zeros((experts * FIRST, part), jnp.float32)
    for q in range(parts):
        chosen = (late & (local // extra == q)).astype(jnp.bfloat16)
        total += jnp.dot(chosen, rows_ref[:, q * part : (q + 1) * part], preferred_element_type=jnp.float32)
    out_ref[:, width:] = (total * late_weight).astype(jnp.bfloat16)


def turn_kernel(groups, in_ref, out_ref):
    copies, rows, slots = out_ref.shape
    piece = rows // groups
    part = copies * piece
    turned = [
        in_ref[:, j * part : (j + 1) * part].astype(jnp.float32).T for j in range(groups)
    ]
    for r in range(copies):
        out_ref[r] = jnp.concatenate(
            [t[r * piece : (r + 1) * piece] for t in turned], axis=0
        ).astype(jnp.bfloat16)


def product_kernel(capacity, parts, moved_ref, hidden_ref, out_ref, total_ref):
    step = pl.program_id(0)
    copies, rows, slots = moved_ref.shape
    places = hidden_ref.shape[1]
    piece = rows // (parts + 1)
    extra = capacity - FIRST
    lane, place = iota((slots, places), 0), iota((slots, places), 1)
    sender, local = lane // FIRST, lane % FIRST
    first = (place == sender * capacity + local).astype(jnp.bfloat16)
    late = place == sender * capacity + FIRST + local % extra
    chosen = [(late & (local // extra == q)).astype(jnp.bfloat16) for q in range(parts)]

    @pl.when(step == 0)
    def _():
        total_ref[...] = jnp.zeros_like(total_ref)

    for r in range(copies):
        moved = moved_ref[r]
        behind = moved[parts * piece :]
        put = jnp.dot(moved[: parts * piece], first, preferred_element_type=jnp.float32)
        put += jnp.concatenate(
            [jnp.dot(behind, c, preferred_element_type=jnp.float32) for c in chosen], axis=0
        )
        total_ref[...] += jnp.dot(
            put.astype(jnp.bfloat16), hidden_ref[r], preferred_element_type=jnp.float32
        )

    @pl.when(step == pl.num_programs(0) - 1)
    def _():
        out_ref[...] = total_ref[...].astype(jnp.bfloat16)


def whole(shape):
    return pl.BlockSpec(shape, lambda *_: (0,) * len(shape))


def dispatch(rows, target, weight, experts, capacity, parts):
    tokens, width = rows.shape
    shape = (experts * FIRST, width + width // parts)
    return pl.pallas_call(
        functools.partial(dispatch_kernel, capacity, parts),
        out_shape=jax.ShapeDtypeStruct(shape, jnp.bfloat16),
        compiler_params=pltpu.CompilerParams(vmem_limit_bytes=VMEM),
        name="dispatch",
    )(rows, target.reshape(1, tokens), weight.reshape(1, tokens))


def turn(arrived, copies, parts):
    slots, width = arrived.shape
    return pl.pallas_call(
        functools.partial(turn_kernel, parts + 1),
        out_shape=jax.ShapeDtypeStruct((copies, width // copies, slots), jnp.bfloat16),
        compiler_params=pltpu.CompilerParams(vmem_limit_bytes=VMEM),
        name="turn",
    )(arrived)


def product(moved, hidden, capacity, parts):
    copies, rows, slots = moved.shape
    places, features = hidden.shape[1:]
    out = (rows // (parts + 1) * parts, features)
    block = 4
    return pl.pallas_call(
        functools.partial(product_kernel, capacity, parts),
        grid=(copies // block,),
        in_specs=[
            pl.BlockSpec((block, rows, slots), lambda i: (i, 0, 0)),
            pl.BlockSpec((block, places, features), lambda i: (i, 0, 0)),
        ],
        out_specs=whole(out),
        out_shape=jax.ShapeDtypeStruct(out, jnp.bfloat16),
        scratch_shapes=[pltpu.VMEM(out, jnp.float32)],
        compiler_params=pltpu.CompilerParams(vmem_limit_bytes=VMEM),
        name="product",
    )(moved, hidden)


def sum_over_micro(partial):
    size = 4
    me = lax.axis_index("micro")
    half = partial.shape[2] // 2
    ahead = [(i, (i + 1) % size) for i in range(size)]
    back = [(i, (i - 1) % size) for i in range(size)]

    def part(k):
        return lax.dynamic_index_in_dim(partial, (me + k) % size, 0, keepdims=False)

    def wide(v):
        return v.astype(jnp.float32)

    own, right, far, left = (part(k) for k in range(size))
    up = lax.ppermute(jnp.concatenate([far[:, :half], right[:, half:]], 1), "micro", ahead)
    down = lax.ppermute(jnp.concatenate([left[:, :half], far[:, half:]], 1), "micro", back)
    up_late = (wide(right[:, :half]) + wide(up[:, :half])).astype(partial.dtype)
    down_late = (wide(left[:, half:]) + wide(down[:, half:])).astype(partial.dtype)
    up_late = lax.ppermute(up_late, "micro", ahead)
    down_late = lax.ppermute(down_late, "micro", back)
    low = wide(own[:, :half]) + wide(up_late) + wide(down[:, :half])
    high = wide(own[:, half:]) + wide(up[:, half:]) + wide(down_late)
    return jnp.concatenate([low, high], 1).astype(partial.dtype)


def shards(grad_rows, routing, route_weight, saved_hidden):
    experts, copies, parts = (lax.axis_size(a) for a in ("expert", "replica", "micro"))
    places, features = saved_hidden.shape
    capacity = places // experts
    hidden = lax.all_gather(saved_hidden, "replica", axis=0, tiled=False)
    sent = dispatch(grad_rows, routing, route_weight, experts, capacity, parts)
    arrived = lax.all_to_all(
        sent.reshape(experts, FIRST, -1), "expert", split_axis=0, concat_axis=0, tiled=True
    )
    turned = turn(arrived.reshape(experts * FIRST, -1), copies, parts)
    moved = lax.all_to_all(turned, "replica", split_axis=0, concat_axis=0, tiled=True)
    partial = product(moved, hidden, capacity, parts)
    part = sum_over_micro(partial.reshape(parts, -1, features))
    piece = part.shape[0]
    out = part.reshape(piece, copies, features // copies).transpose(1, 0, 2)
    out = lax.all_to_all(out, "replica", split_axis=0, concat_axis=0, tiled=True)
    out = out.reshape(copies * piece, features // copies).T
    return out.astype(jnp.float32)[None]


def solution(mesh):
    rows = P(("expert", "replica", "micro"), None)
    return jax.shard_map(
        shards,
        mesh=mesh,
        in_specs=(rows, rows, rows, rows),
        out_specs=P("expert", "replica", "micro"),
        check_vma=False,
    )
```

time: 445 us -> 217 us (0.49)
  the two profiles are of different devices: /device:TPU:2 before, /device:TPU:1 now
where the time goes in v1:
time: 217 us; the launch traced here: 216 us
  blocking collectives  84 us (39%)
  waiting for transfers between devices  67.8 us (31%)
  starting transfers between devices  37 us (17%)
  between operations  13.6 us (6%)
  Pallas kernels  9.59 us (4%)
  local copies, waits for them, and re-layouts  4.09 us (2%)
    all_to_all x1, blocking collectives, shards(): lax.all_to_all(sent.reshape(experts, FIRST, -1), 'expert', split_axis=0,...  72.1 us
    all_to_all x1, waiting for transfers between devices, shards(): lax.all_to_all(turned, 'replica', split_axis=0, concat_axis=0, tiled=True)  30.2 us
    ppermute x1, waiting for transfers between devices, sum_over_micro(): down_late = lax.ppermute(down_late, 'micro', back)  14.8 us
    ppermute x1, waiting for transfers between devices, sum_over_micro(): lax.ppermute(jnp.concatenate([left[:, :half], far[:, half:]], 1), 'micro'...  14.5 us
    ppermute x1, starting transfers between devices, sum_over_micro(): up_late = lax.ppermute(up_late, 'micro', ahead)  13.1 us
    ppermute x1, starting transfers between devices, sum_over_micro(): lax.ppermute(jnp.concatenate([far[:, :half], right[:, half:]], 1), 'micro...  12.5 us
    all_to_all x1, blocking collectives, shards(): lax.all_to_all(out, 'replica', split_axis=0, concat_axis=0, tiled=True)  12 us
    pallas_call x1, Pallas kernels, product(): pl.pallas_call(functools.partial(product_kernel, capacity, parts), grid=(...  7.39 us
  transfers between devices with their start and end apart: 6, of which 5 were waited for; matrix products, arithmetic and copies ran while one was open for 0% of the time, Pallas kernels for 1%

profile of v1, /device:TPU:1, one launch (start us, length us, event | category | flops | bytes accessed | tf_op | source)
XLA Modules:
  0.0 216.3 jit_solution(6093789485439199451)
XLA Ops:
  6.5 0.0 all-gather.3.cloned.1.call-start
  6.5 0.7 all-gather.3.cloned.1.call-update
  7.3 0.0 copy-start
  7.3 1.2 copy-done
  8.4 0.0 copy-start.1
  8.4 0.7 copy-done.1
  9.1 0.0 copy-start.2
  9.1 0.7 copy-done.2
  9.7 0.8 dispatch.1
  10.5 72.1 %all_to_all.15 = bf16[16,8,4480]{2,1,0:T(8,128)(2,1)S(1)} all-to-all(bf16[16,8,4480]{2,1,0:T(8,128)(2,1)S(1)} %bitcast.22), channel_id=1, replica_groups=mesh['expert'=16,'replica'=16,'micro'=4] {'expert'}, dimensions={0} | all-to-all | bytes 2293760 | tf_op jit(solution)/shard_map/all_to_all | solution.py:167
  82.6 1.4 turn.1
  84.0 4.0 %all-to-all-start.1 = ((bf16[16,280,128]{2,1,0:T(8,128)(2,1)}), bf16[16,280,128]{2,1,0:T(8,128)(2,1)S(1)}, u32[]{:S(2)}, u32[]{:S(2)}) async-start(bf16[16,280,128]{2,1,0:T(8,128)(2,1)} %turn.1), calls=%async_computation.1 | async-start | bytes 2293760 | tf_op jit(solution)/shard_map/all_to_all | solution.py:171
  88.1 30.2 %all-to-all-done.1.moved_ref = bf16[16,280,128]{2,1,0:T(8,128)(2,1)S(1)} async-done(((bf16[16,280,128]{2,1,0:T(8,128)(2,1)}), bf16[16,280,128]{2,1,0:T(8,128)(2,1)S(1)}, u32[]{:S(2)}, u32[]{:S(2)}) %all-to-all-start.1) | async-done | bytes 1146912 | tf_op jit(solution)/shard_map/all_to_all | solution.py:171
  118.2 6.2 %all-gather.3.cloned.1.call-done = bf16[2560,1024]{1,0:T(8,128)(2,1)} async-done(((bf16[160,1024]{1,0:T(8,128)(2,1)}), bf16[2560,1024]{1,0:T(8,128)(2,1)}) %all-gather.3.cloned.1.call-update) | async-done | bytes 5242896 | tf_op jit(solution)/shard_map/all_gather | solution.py:165
  124.5 7.4 %product.1 = bf16[224,1024]{1,0:T(8,128)(2,1)S(1)} custom-call(bf16[16,280,128]{2,1,0:T(8,128)(2,1)S(1)} %all-to-all-done.1.moved_ref, bf16[16,160,1024]{2,1,0:T(8,128)(2,1)} %bitcast.27), custom_call_target="tpu_custom_call" | custom-call | tf_op jit(solution)/shard_map/product/pallas_call | solution.py:121
  132.0 12.5 %collective-permute-start = (bf16[56,1024]{1,0:T(8,128)(2,1)S(1)}, bf16[56,1024]{1,0:T(8,128)(2,1)S(1)}, u32[]{:S(2)}, u32[]{:S(2)}) collective-permute-start(bf16[56,1024]{1,0:T(8,128)(2,1)S(1)} %pad_maximum_fusion), channel_id=1, source_target_pairs={{0,1},{1,2},{2,3},{3,0},{4,5},{5,6},{6,7},{7,4},{8,9},{9,10},{10,1... | collective-permute-start | bytes 344072 | tf_op jit(solution)/shard_map/ppermute | solution.py:150
  144.5 3.4 %collective-permute-start.2 = (bf16[56,1024]{1,0:T(8,128)(2,1)S(1)}, bf16[56,1024]{1,0:T(8,128)(2,1)S(1)}, u32[]{:S(2)}, u32[]{:S(2)}) collective-permute-start(bf16[56,1024]{1,0:T(8,128)(2,1)S(1)} %pad_maximum_fusion.1), channel_id=1, source_target_pairs={{0,3},{1,0},{2,1},{3,2},{4,7},{5,4},{6,5},{7,6},{8,11},{9,8},{10,9... | collective-permute-start | bytes 344072 | tf_op jit(solution)/shard_map/ppermute | solution.py:151
  147.9 1.3 collective-permute-done
  149.2 13.1 %collective-permute-start.1 = (bf16[56,512]{1,0:T(8,128)(2,1)S(1)}, bf16[56,512]{1,0:T(8,128)(2,1)S(1)}, u32[]{:S(2)}, u32[]{:S(2)}) collective-permute-start(bf16[56,512]{1,0:T(8,128)(2,1)S(1)} %add_convert_fusion.3), channel_id=1, source_target_pairs={{0,1},{1,2},{2,3},{3,0},{4,5},{5,6},{6,7},{7,4},{8,9},{9,10},{10,1... | collective-permute-start | bytes 172040 | tf_op jit(solution)/shard_map/ppermute | solution.py:154
  162.3 14.5 %collective-permute-done.2 = bf16[56,1024]{1,0:T(8,128)(2,1)S(1)} collective-permute-done((bf16[56,1024]{1,0:T(8,128)(2,1)S(1)}, bf16[56,1024]{1,0:T(8,128)(2,1)S(1)}, u32[]{:S(2)}, u32[]{:S(2)}) %collective-permute-start.2) | collective-permute-done | bytes 114720 | tf_op jit(solution)/shard_map/ppermute | solution.py:151
  176.9 4.0 %collective-permute-start.3 = (bf16[56,512]{1,0:T(8,128)(2,1)S(1)}, bf16[56,512]{1,0:T(8,128)(2,1)S(1)}, u32[]{:S(2)}, u32[]{:S(2)}) collective-permute-start(bf16[56,512]{1,0:T(8,128)(2,1)S(1)} %add_convert_fusion.1), channel_id=1, source_target_pairs={{0,3},{1,0},{2,1},{3,2},{4,7},{5,4},{6,5},{7,6},{8,11},{9,8},{10,9... | collective-permute-start | bytes 172040 | tf_op jit(solution)/shard_map/ppermute | solution.py:155
  180.9 0.0 collective-permute-done.1
  180.9 14.8 %collective-permute-done.3 = bf16[56,512]{1,0:T(8,128)(2,1)S(1)} collective-permute-done((bf16[56,512]{1,0:T(8,128)(2,1)S(1)}, bf16[56,512]{1,0:T(8,128)(2,1)S(1)}, u32[]{:S(2)}, u32[]{:S(2)}) %collective-permute-start.3) | collective-permute-done | bytes 57376 | tf_op jit(solution)/shard_map/ppermute | solution.py:155
  195.8 0.1 add_convert_fusion.2
  195.8 0.1 concatenate.18
  195.9 0.1 concatenate.17
  196.1 0.1 copy.6
  196.2 0.2 reshape.31
  196.4 12.0 %all_to_all.16 = bf16[16,2,1792]{2,1,0:T(2,128)(2,1)S(1)} all-to-all(bf16[16,2,1792]{2,1,0:T(2,128)(2,1)S(1)} %reshape.31), channel_id=1, replica_groups=mesh['expert'=16,'replica'=16,'micro'=4] {'replica'}, dimensions={0} | all-to-all | bytes 229376 | tf_op jit(solution)/shard_map/all_to_all | solution.py:176
  208.3 0.2 reshape.32
  208.6 0.9 copy.8
  (10 shorter events, 0.2 us)
Async XLA Ops:
  6.5 117.9 %all-gather.3.cloned.1.call-start = ((), (), s32[]{:S(2)}) async-start(), calls=%async_computation.3 | async-start | bytes 5570560 | tf_op jit(solution)/shard_map/all_gather | solution.py:165
  7.3 1.2 copy-start
  8.4 0.7 copy-start.1
  9.1 0.7 copy-start.2
  84.0 34.2 %all-to-all-start.1 = ((bf16[16,280,128]{2,1,0:T(8,128)(2,1)}), bf16[16,280,128]{2,1,0:T(8,128)(2,1)S(1)}, u32[]{:S(2)}, u32[]{:S(2)}) async-start(bf16[16,280,128]{2,1,0:T(8,128)(2,1)} %turn.1), calls=%async_computation.1 | async-start | bytes 2293760 | tf_op jit(solution)/shard_map/all_to_all | solution.py:171
  132.0 17.3 %collective-permute-start = (bf16[56,1024]{1,0:T(8,128)(2,1)S(1)}, bf16[56,1024]{1,0:T(8,128)(2,1)S(1)}, u32[]{:S(2)}, u32[]{:S(2)}) collective-permute-start(bf16[56,1024]{1,0:T(8,128)(2,1)S(1)} %pad_maximum_fusion), channel_id=1, source_target_pairs={{0,1},{1,2},{2,3},{3,0},{4,5},{5,6},{6,7},{7,4},{8,9},{9,10},{10,1... | collective-permute-start | bytes 344072 | tf_op jit(solution)/shard_map/ppermute | solution.py:150
  144.5 32.4 %collective-permute-start.2 = (bf16[56,1024]{1,0:T(8,128)(2,1)S(1)}, bf16[56,1024]{1,0:T(8,128)(2,1)S(1)}, u32[]{:S(2)}, u32[]{:S(2)}) collective-permute-start(bf16[56,1024]{1,0:T(8,128)(2,1)S(1)} %pad_maximum_fusion.1), channel_id=1, source_target_pairs={{0,3},{1,0},{2,1},{3,2},{4,7},{5,4},{6,5},{7,6},{8,11},{9,8},{10,9... | collective-permute-start | bytes 344072 | tf_op jit(solution)/shard_map/ppermute | solution.py:151
  149.2 31.7 %collective-permute-start.1 = (bf16[56,512]{1,0:T(8,128)(2,1)S(1)}, bf16[56,512]{1,0:T(8,128)(2,1)S(1)}, u32[]{:S(2)}, u32[]{:S(2)}) collective-permute-start(bf16[56,512]{1,0:T(8,128)(2,1)S(1)} %add_convert_fusion.3), channel_id=1, source_target_pairs={{0,1},{1,2},{2,3},{3,0},{4,5},{5,6},{6,7},{7,4},{8,9},{9,10},{10,1... | collective-permute-start | bytes 172040 | tf_op jit(solution)/shard_map/ppermute | solution.py:154
  176.9 18.9 %collective-permute-start.3 = (bf16[56,512]{1,0:T(8,128)(2,1)S(1)}, bf16[56,512]{1,0:T(8,128)(2,1)S(1)}, u32[]{:S(2)}, u32[]{:S(2)}) collective-permute-start(bf16[56,512]{1,0:T(8,128)(2,1)S(1)} %add_convert_fusion.1), channel_id=1, source_target_pairs={{0,3},{1,0},{2,1},{3,2},{4,7},{5,4},{6,5},{7,6},{8,11},{9,8},{10,9... | collective-permute-start | bytes 172040 | tf_op jit(solution)/shard_map/ppermute | solution.py:155
Sparse Core Ops, SparseCore 0:
  11.5 112.8 all-gather.2

commit v2 on v1

--- a/solution.py
+++ b/solution.py
@@ -5,10 +5,14 @@
 from jax import lax
 from jax.experimental import pallas as pl
 from jax.experimental.pallas import tpu as pltpu
+from jax.sharding import Mesh
 from jax.sharding import PartitionSpec as P
 
 FIRST = 8
 VMEM = 48 * 1024 * 1024
+
+
+REPLICA = ("y", "x")
 
 
 def iota(shape, dimension):
@@ -56,40 +60,75 @@
         ).astype(jnp.bfloat16)
 
 
-def product_kernel(capacity, parts, moved_ref, hidden_ref, out_ref, total_ref):
-    step = pl.program_id(0)
+def order_kernel(capacity, hidden_ref, out_ref):
+    places = hidden_ref.shape[0]
+    extra = capacity - FIRST
+    senders = places // capacity
+    row, place = iota((places, places), 0), iota((places, places), 1)
+    late = row - senders * FIRST
+    source = jnp.where(
+        late < 0,
+        row // FIRST * capacity + row % FIRST,
+        late // extra * capacity + FIRST + late % extra,
+    )
+    chosen = (source == place).astype(jnp.bfloat16)
+    out_ref[...] = jnp.dot(
+        chosen, hidden_ref[...], preferred_element_type=jnp.float32
+    ).astype(jnp.bfloat16)
+
+
+def product_kernel(parts, extra, spot_ref, moved_ref, *refs):
+    *hidden, out_ref = refs
     copies, rows, slots = moved_ref.shape
-    places = hidden_ref.shape[1]
+    side = hidden[0].shape[0]
     piece = rows // (parts + 1)
-    extra = capacity - FIRST
-    lane, place = iota((slots, places), 0), iota((slots, places), 1)
+    senders = slots // FIRST
+    lane, place = iota((slots, slots), 0), iota((slots, slots), 1)
     sender, local = lane // FIRST, lane % FIRST
-    first = (place == sender * capacity + local).astype(jnp.bfloat16)
-    late = place == sender * capacity + FIRST + local % extra
-    chosen = [(late & (local // extra == q)).astype(jnp.bfloat16) for q in range(parts)]
-
-    @pl.when(step == 0)
-    def _():
-        total_ref[...] = jnp.zeros_like(total_ref)
-
-    for r in range(copies):
-        moved = moved_ref[r]
-        behind = moved[parts * piece :]
-        put = jnp.dot(moved[: parts * piece], first, preferred_element_type=jnp.float32)
-        put += jnp.concatenate(
-            [jnp.dot(behind, c, preferred_element_type=jnp.float32) for c in chosen], axis=0
+    goes = [
+        jnp.concatenate(
+            [
+                (local // extra == q) & (place == r * senders * extra + sender * extra + local % extra)
+                for r in range(side)
+            ],
+            axis=0,
+        ).astype(jnp.bfloat16)
+        for q in range(parts)
+    ]
+    total = jnp.zeros(out_ref.shape, jnp.float32)
+    for k in range(side):
+        y = lax.rem(spot_ref[0] + k, side)
+        moved = [moved_ref[y * side + lax.rem(spot_ref[1] + j, side)] for j in range(side)]
+        behind = jnp.concatenate(
+            [m[parts * piece :].astype(jnp.float32) for m in moved], axis=1
+        ).astype(jnp.bfloat16)
+        late = [jnp.dot(behind, g, preferred_element_type=jnp.float32) for g in goes]
+        left = [m[: parts * piece] for m in moved]
+        left.append(jnp.concatenate(late, axis=0).astype(jnp.bfloat16))
+        if k == 2:
+            low, high = hidden[2], hidden[3]
+            cut = slots - low.shape[1]
+            first = [part for j in range(side) for part in (low[j], high[j][:cut])]
+            last = [high[j][cut:] for j in range(side)]
+        else:
+            held = hidden[k if k < 2 else k + 1]
+            first = [held[j][:slots] for j in range(side)]
+            last = [held[j][slots:] for j in range(side)]
+        total += jnp.dot(
+            jnp.concatenate(left, axis=1),
+            jnp.concatenate(first + last, axis=0),
+            preferred_element_type=jnp.float32,
         )
-        total_ref[...] += jnp.dot(
-            put.astype(jnp.bfloat16), hidden_ref[r], preferred_element_type=jnp.float32
-        )
-
-    @pl.when(step == pl.num_programs(0) - 1)
-    def _():
-        out_ref[...] = total_ref[...].astype(jnp.bfloat16)
-
-
-def whole(shape):
-    return pl.BlockSpec(shape, lambda *_: (0,) * len(shape))
+    out_ref[...] = total.astype(jnp.bfloat16)
+
+
+def order(hidden, capacity):
+    return pl.pallas_call(
+        functools.partial(order_kernel, capacity),
+        out_shape=jax.ShapeDtypeStruct(hidden.shape, jnp.bfloat16),
+        compiler_params=pltpu.CompilerParams(vmem_limit_bytes=VMEM),
+        name="order",
+    )(hidden)
 
 
 def dispatch(rows, target, weight, experts, capacity, parts):
@@ -113,24 +152,19 @@
     )(arrived)
 
 
-def product(moved, hidden, capacity, parts):
+def product(moved, hidden, spot, capacity, parts):
     copies, rows, slots = moved.shape
-    places, features = hidden.shape[1:]
+    features = hidden[0].shape[2]
     out = (rows // (parts + 1) * parts, features)
-    block = 4
-    return pl.pallas_call(
-        functools.partial(product_kernel, capacity, parts),
-        grid=(copies // block,),
-        in_specs=[
-            pl.BlockSpec((block, rows, slots), lambda i: (i, 0, 0)),
-            pl.BlockSpec((block, places, features), lambda i: (i, 0, 0)),
-        ],
-        out_specs=whole(out),
+    inside = pl.BlockSpec(memory_space=pltpu.VMEM)
+    return pl.pallas_call(
+        functools.partial(product_kernel, parts, capacity - FIRST),
+        in_specs=[pl.BlockSpec(memory_space=pltpu.SMEM)] + [inside] * (1 + len(hidden)),
+        out_specs=inside,
         out_shape=jax.ShapeDtypeStruct(out, jnp.bfloat16),
-        scratch_shapes=[pltpu.VMEM(out, jnp.float32)],
         compiler_params=pltpu.CompilerParams(vmem_limit_bytes=VMEM),
         name="product",
-    )(moved, hidden)
+    )(spot, moved, *hidden)
 
 
 def sum_over_micro(partial):
@@ -158,32 +192,57 @@
     return jnp.concatenate([low, high], 1).astype(partial.dtype)
 
 
+def ring_gather(block, axis):
+    size = lax.axis_size(axis)
+    ahead = [(i, (i + 1) % size) for i in range(size)]
+    back = [(i, (i - 1) % size) for i in range(size)]
+    half = block.shape[-2] // 2
+    behind = lax.ppermute(block, axis, ahead)
+    before = lax.ppermute(block, axis, back)
+    low = lax.ppermute(behind[..., :half, :], axis, ahead)
+    high = lax.ppermute(before[..., half:, :], axis, back)
+    return block, before, low, high, behind
+
+
+def gather_hidden(block):
+    own, before, low, high, behind = ring_gather(block, "x")
+    row = jnp.stack([own, before, jnp.concatenate([low, high], axis=0), behind])
+    return ring_gather(row, "y")
+
+
 def shards(grad_rows, routing, route_weight, saved_hidden):
-    experts, copies, parts = (lax.axis_size(a) for a in ("expert", "replica", "micro"))
+    experts, copies, parts = (lax.axis_size(a) for a in ("expert", REPLICA, "micro"))
     places, features = saved_hidden.shape
     capacity = places // experts
-    hidden = lax.all_gather(saved_hidden, "replica", axis=0, tiled=False)
+    hidden = order(saved_hidden, capacity)
     sent = dispatch(grad_rows, routing, route_weight, experts, capacity, parts)
+    hidden = gather_hidden(hidden)
     arrived = lax.all_to_all(
         sent.reshape(experts, FIRST, -1), "expert", split_axis=0, concat_axis=0, tiled=True
     )
     turned = turn(arrived.reshape(experts * FIRST, -1), copies, parts)
-    moved = lax.all_to_all(turned, "replica", split_axis=0, concat_axis=0, tiled=True)
-    partial = product(moved, hidden, capacity, parts)
+    moved = lax.all_to_all(turned, REPLICA, split_axis=0, concat_axis=0, tiled=True)
+    spot = jnp.stack([lax.axis_index("y"), lax.axis_index("x")])
+    partial = product(moved, hidden, spot, capacity, parts)
     part = sum_over_micro(partial.reshape(parts, -1, features))
     piece = part.shape[0]
     out = part.reshape(piece, copies, features // copies).transpose(1, 0, 2)
-    out = lax.all_to_all(out, "replica", split_axis=0, concat_axis=0, tiled=True)
+    out = lax.all_to_all(out, REPLICA, split_axis=0, concat_axis=0, tiled=True)
     out = out.reshape(copies * piece, features // copies).T
     return out.astype(jnp.float32)[None]
 
 
 def solution(mesh):
-    rows = P(("expert", "replica", "micro"), None)
+    experts, copies, parts = (mesh.shape[a] for a in ("expert", "replica", "micro"))
+    side = 4
+    split = Mesh(
+        mesh.devices.reshape(experts, copies // side, side, parts), ("expert", "y", "x", "micro")
+    )
+    rows = P(("expert", "y", "x", "micro"), None)
     return jax.shard_map(
         shards,
-        mesh=mesh,
+        mesh=split,
         in_specs=(rows, rows, rows, rows),
-        out_specs=P("expert", "replica", "micro"),
+        out_specs=P("expert", REPLICA, "micro"),
         check_vma=False,
     )

time: 217 us -> 192 us (0.88)
  the two profiles are of different devices: /device:TPU:1 before, /device:TPU:2 now
where the time goes in v2:
time: 192 us; the launch traced here: 191 us
  starting transfers between devices  81.8 us (43%)
  waiting for transfers between devices  79.7 us (42%)
  blocking collectives  13.2 us (7%)
  local copies, waits for them, and re-layouts  9.11 us (5%)
  Pallas kernels  6.34 us (3%)
    ppermute x2, waiting for transfers between devices, ring_gather(): low = lax.ppermute(behind[..., :half, :], axis, ahead)  19.3 us
    ppermute x1, waiting for transfers between devices, sum_over_micro(): lax.ppermute(jnp.concatenate([far[:, :half], right[:, half:]], 1), 'micro...  17.3 us
    ppermute x1, waiting for transfers between devices, sum_over_micro(): down_late = lax.ppermute(down_late, 'micro', back)  15.2 us
    ppermute x1, starting transfers between devices, sum_over_micro(): lax.ppermute(jnp.concatenate([far[:, :half], right[:, half:]], 1), 'micro...  15.1 us
    all_to_all x1, waiting for transfers between devices, shards(): lax.all_to_all(sent.reshape(experts, FIRST, -1), 'expert', split_axis=0,...  14.7 us
    ppermute x1, starting transfers between devices, sum_over_micro(): up_late = lax.ppermute(up_late, 'micro', ahead)  13.4 us
    all_to_all x1, blocking collectives, shards(): out = lax.all_to_all(out, REPLICA, split_axis=0, concat_axis=0, tiled=True)  13.2 us
    all_to_all x1, starting transfers between devices, shards(): lax.all_to_all(sent.reshape(experts, FIRST, -1), 'expert', split_axis=0,...  12.8 us
  transfers between devices with their start and end apart: 14, of which 10 were waited for; matrix products, arithmetic and copies ran while one was open for 2% of the time, Pallas kernels for 0%

profile of v2, /device:TPU:2, one launch (start us, length us, event | category | flops | bytes accessed | tf_op | source)
XLA Modules:
  0.0 191.0 jit_solution(8086174801460189144)
XLA Ops:
  0.0 1.2 copy-done.1
  1.2 0.7 copy-done.3
  1.8 0.7 copy-done.4
  2.5 1.8 dispatch.1
  4.3 12.8 %all-to-all-start = ((bf16[16,8,4480]{2,1,0:T(8,128)(2,1)}), bf16[16,8,4480]{2,1,0:T(8,128)(2,1)S(1)}, u32[]{:S(2)}, u32[]{:S(2)}) async-start(bf16[16,8,4480]{2,1,0:T(8,128)(2,1)} %bitcast.4), calls=%async_computation | async-start | bytes 2293760 | tf_op jit(solution)/shard_map/all_to_all | solution.py:220
  17.1 0.2 order.1
  17.3 6.2 %collective-permute-start = (bf16[160,1024]{1,0:T(8,128)(2,1)S(1)}, bf16[160,1024]{1,0:T(8,128)(2,1)S(1)}, u32[]{:S(2)}, u32[]{:S(2)}) collective-permute-start(bf16[160,1024]{1,0:T(8,128)(2,1)S(1)} %order.1), channel_id=1, source_target_pairs={{0,12},{4,0},{8,4},{12,8},{1,13},{5,1},{9,5},{13,9},{2,14},{6,2},{... | collective-permute-start | bytes 983048 | tf_op jit(solution)/shard_map/ppermute | solution.py:201
  23.5 1.9 %collective-permute-start.1 = (bf16[160,1024]{1,0:T(8,128)(2,1)S(1)}, bf16[160,1024]{1,0:T(8,128)(2,1)S(1)}, u32[]{:S(2)}, u32[]{:S(2)}) collective-permute-start(bf16[160,1024]{1,0:T(8,128)(2,1)S(1)} %order.1), channel_id=1, source_target_pairs={{0,4},{4,8},{8,12},{12,0},{1,5},{5,9},{9,13},{13,1},{2,6},{6,10},{... | collective-permute-start | bytes 983048 | tf_op jit(solution)/shard_map/ppermute | solution.py:200
  25.4 5.5 %collective-permute-done = bf16[160,1024]{1,0:T(8,128)(2,1)S(1)} collective-permute-done((bf16[160,1024]{1,0:T(8,128)(2,1)S(1)}, bf16[160,1024]{1,0:T(8,128)(2,1)S(1)}, u32[]{:S(2)}, u32[]{:S(2)}) %collective-permute-start) | collective-permute-done | bytes 327712 | tf_op jit(solution)/shard_map/ppermute | solution.py:201
  30.9 4.4 %collective-permute-start.3 = (bf16[80,1024]{1,0:T(8,128)(2,1)S(1)}, bf16[80,1024]{1,0:T(8,128)(2,1)S(1)}, u32[]{:S(2)}, u32[]{:S(2)}) collective-permute-start(bf16[80,1024]{1,0:T(8,128)(2,1)S(1)} %slice.65), channel_id=1, source_target_pairs={{0,12},{4,0},{8,4},{12,8},{1,13},{5,1},{9,5},{13,9},{2,14},{6,2},{... | collective-permute-start | bytes 491528 | tf_op jit(solution)/shard_map/ppermute | solution.py:203
  35.3 0.0 collective-permute-done.1
  35.3 1.9 %collective-permute-start.2 = (bf16[80,1024]{1,0:T(8,128)(2,1)S(1)}, bf16[80,1024]{1,0:T(8,128)(2,1)S(1)}, u32[]{:S(2)}, u32[]{:S(2)}) collective-permute-start(bf16[80,1024]{1,0:T(8,128)(2,1)S(1)} %slice.64), channel_id=1, source_target_pairs={{0,4},{4,8},{8,12},{12,0},{1,5},{5,9},{9,13},{13,1},{2,6},{6,10},{... | collective-permute-start | bytes 491528 | tf_op jit(solution)/shard_map/ppermute | solution.py:202
  37.2 1.1 collective-permute-done.3
  38.4 4.2 %collective-permute-done.2 = bf16[80,1024]{1,0:T(8,128)(2,1)S(1)} collective-permute-done((bf16[80,1024]{1,0:T(8,128)(2,1)S(1)}, bf16[80,1024]{1,0:T(8,128)(2,1)S(1)}, u32[]{:S(2)}, u32[]{:S(2)}) %collective-permute-start.2) | collective-permute-done | bytes 163872 | tf_op jit(solution)/shard_map/ppermute | solution.py:202
  42.6 0.2 pad_maximum_fusion.refs_0_
  42.8 2.2 %collective-permute-start.5 = (bf16[4,160,1024]{2,1,0:T(8,128)(2,1)S(1)}, bf16[4,160,1024]{2,1,0:T(8,128)(2,1)}, u32[]{:S(2)}, u32[]{:S(2)}) collective-permute-start(bf16[4,160,1024]{2,1,0:T(8,128)(2,1)S(1)} %pad_maximum_fusion.refs_0_), channel_id=1, source_target_pairs={{0,16},{16,32},{32,48},{48,0},{1,17},{17,33},{33,49},{49,1},{2,18}... | collective-permute-start | bytes 3932168 | tf_op jit(solution)/shard_map/ppermute | solution.py:200
  45.0 4.8 %collective-permute-start.4 = (bf16[4,160,1024]{2,1,0:T(8,128)(2,1)S(1)}, bf16[4,160,1024]{2,1,0:T(8,128)(2,1)}, u32[]{:S(2)}, u32[]{:S(2)}) collective-permute-start(bf16[4,160,1024]{2,1,0:T(8,128)(2,1)S(1)} %pad_maximum_fusion.refs_0_), channel_id=1, source_target_pairs={{0,48},{16,0},{32,16},{48,32},{1,49},{17,1},{33,17},{49,33},{2,50}... | collective-permute-start | bytes 3932168 | tf_op jit(solution)/shard_map/ppermute | solution.py:201
  49.9 14.7 %all-to-all-done = bf16[16,8,4480]{2,1,0:T(8,128)(2,1)S(1)} async-done(((bf16[16,8,4480]{2,1,0:T(8,128)(2,1)}), bf16[16,8,4480]{2,1,0:T(8,128)(2,1)S(1)}, u32[]{:S(2)}, u32[]{:S(2)}) %all-to-all-start) | async-done | bytes 1146912 | tf_op jit(solution)/shard_map/all_to_all | solution.py:220
  64.5 0.4 turn.1
  64.9 1.0 copy-done
  65.9 7.7 %all-to-all-start.1 = ((bf16[16,280,128]{2,1,0:T(8,128)(2,1)}), bf16[16,280,128]{2,1,0:T(8,128)(2,1)S(1)}, u32[]{:S(2)}, u32[]{:S(2)}) async-start(bf16[16,280,128]{2,1,0:T(8,128)(2,1)} %copy-done), calls=%async_computation.1 | async-start | bytes 2293760 | tf_op jit(solution)/shard_map/all_to_all | solution.py:224
  73.6 1.5 collective-permute-done.5.refs_4_
  75.1 2.0 %slice.66 = bf16[4,80,1024]{2,1,0:T(8,128)(2,1)} slice(bf16[4,160,1024]{2,1,0:T(8,128)(2,1)} %collective-permute-done.5.refs_4_), slice={[0:4], [0:80], [0:1024]} | slice | bytes 1310720 | tf_op jit(solution)/shard_map/slice | solution.py:202
  77.0 1.9 %collective-permute-start.6 = (bf16[4,80,1024]{2,1,0:T(8,128)(2,1)}, bf16[4,80,1024]{2,1,0:T(8,128)(2,1)S(1)}, u32[]{:S(2)}, u32[]{:S(2)}) collective-permute-start(bf16[4,80,1024]{2,1,0:T(8,128)(2,1)} %slice.66), channel_id=1, source_target_pairs={{0,16},{16,32},{32,48},{48,0},{1,17},{17,33},{33,49},{49,1},{2,18}... | collective-permute-start | bytes 1966088 | tf_op jit(solution)/shard_map/ppermute | solution.py:202
  79.0 2.6 %collective-permute-done.4.refs_1_ = bf16[4,160,1024]{2,1,0:T(8,128)(2,1)} collective-permute-done((bf16[4,160,1024]{2,1,0:T(8,128)(2,1)S(1)}, bf16[4,160,1024]{2,1,0:T(8,128)(2,1)}, u32[]{:S(2)}, u32[]{:S(2)}) %collective-permute-start.4) | collective-permute-done | bytes 1310752 | tf_op jit(solution)/shard_map/ppermute | solution.py:201
  81.5 2.0 %slice.67 = bf16[4,80,1024]{2,1,0:T(8,128)(2,1)} slice(bf16[4,160,1024]{2,1,0:T(8,128)(2,1)} %collective-permute-done.4.refs_1_), slice={[0:4], [80:160], [0:1024]} | slice | bytes 1310720 | tf_op jit(solution)/shard_map/slice | solution.py:203
  83.5 5.7 %collective-permute-start.7 = (bf16[4,80,1024]{2,1,0:T(8,128)(2,1)}, bf16[4,80,1024]{2,1,0:T(8,128)(2,1)}, u32[]{:S(2)}, u32[]{:S(2)}) collective-permute-start(bf16[4,80,1024]{2,1,0:T(8,128)(2,1)} %slice.67), channel_id=1, source_target_pairs={{0,48},{16,0},{32,16},{48,32},{1,49},{17,1},{33,17},{49,33},{2,50}... | collective-permute-start | bytes 1966088 | tf_op jit(solution)/shard_map/ppermute | solution.py:203
  89.3 0.1 pad_add_fusion.spot_ref
  89.3 15.1 %collective-permute-done.6.refs_2_ = bf16[4,80,1024]{2,1,0:T(8,128)(2,1)S(1)} collective-permute-done((bf16[4,80,1024]{2,1,0:T(8,128)(2,1)}, bf16[4,80,1024]{2,1,0:T(8,128)(2,1)S(1)}, u32[]{:S(2)}, u32[]{:S(2)}) %collective-permute-start.6) | collective-permute-done | bytes 655392 | tf_op jit(solution)/shard_map/ppermute | solution.py:202
  104.4 0.0 collective-permute-done.7.refs_3_
  104.4 0.0 all-to-all-done.1.moved_ref
  104.4 4.0 %product.1 = bf16[224,1024]{1,0:T(8,128)(2,1)S(1)} custom-call(s32[2]{0:T(128)S(1)} %pad_add_fusion.spot_ref, bf16[16,280,128]{2,1,0:T(8,128)(2,1)S(1)} %all-to-all-done.1.moved_ref, bf16[4,160,1024]{2,1,0:T(8,128)(2,1)S(1)} %pad_maximum_fusion.refs_0_, bf16[4,160,1024]{2,1,0:T(8,128)(2,1)} %collective-permute-done.4.refs_1_, ...), custom_call_target="tpu_custom_call" | custom-call | tf_op jit(solution)/shard_map/product/pallas_call | solution.py:160
  108.5 15.1 %collective-permute-start.8 = (bf16[56,1024]{1,0:T(8,128)(2,1)S(1)}, bf16[56,1024]{1,0:T(8,128)(2,1)S(1)}, u32[]{:S(2)}, u32[]{:S(2)}) collective-permute-start(bf16[56,1024]{1,0:T(8,128)(2,1)S(1)} %pad_maximum_fusion.1), channel_id=1, source_target_pairs={{0,1},{1,2},{2,3},{3,0},{4,5},{5,6},{6,7},{7,4},{8,9},{9,10},{10,1... | collective-permute-start | bytes 344072 | tf_op jit(solution)/shard_map/ppermute | solution.py:184
  123.7 1.9 %collective-permute-start.10 = (bf16[56,1024]{1,0:T(8,128)(2,1)S(1)}, bf16[56,1024]{1,0:T(8,128)(2,1)S(1)}, u32[]{:S(2)}, u32[]{:S(2)}) collective-permute-start(bf16[56,1024]{1,0:T(8,128)(2,1)S(1)} %pad_maximum_fusion.2), channel_id=1, source_target_pairs={{0,3},{1,0},{2,1},{3,2},{4,7},{5,4},{6,5},{7,6},{8,11},{9,8},{10,9... | collective-permute-start | bytes 344072 | tf_op jit(solution)/shard_map/ppermute | solution.py:185
  125.6 17.3 %collective-permute-done.8 = bf16[56,1024]{1,0:T(8,128)(2,1)S(1)} collective-permute-done((bf16[56,1024]{1,0:T(8,128)(2,1)S(1)}, bf16[56,1024]{1,0:T(8,128)(2,1)S(1)}, u32[]{:S(2)}, u32[]{:S(2)}) %collective-permute-start.8) | collective-permute-done | bytes 114720 | tf_op jit(solution)/shard_map/ppermute | solution.py:184
  142.9 13.4 %collective-permute-start.9 = (bf16[56,512]{1,0:T(8,128)(2,1)S(1)}, bf16[56,512]{1,0:T(8,128)(2,1)S(1)}, u32[]{:S(2)}, u32[]{:S(2)}) collective-permute-start(bf16[56,512]{1,0:T(8,128)(2,1)S(1)} %add_convert_fusion.3), channel_id=1, source_target_pairs={{0,1},{1,2},{2,3},{3,0},{4,5},{5,6},{6,7},{7,4},{8,9},{9,10},{10,1... | collective-permute-start | bytes 172040 | tf_op jit(solution)/shard_map/ppermute | solution.py:188
  156.3 0.0 collective-permute-done.10
  156.4 1.9 %collective-permute-start.11 = (bf16[56,512]{1,0:T(8,128)(2,1)S(1)}, bf16[56,512]{1,0:T(8,128)(2,1)S(1)}, u32[]{:S(2)}, u32[]{:S(2)}) collective-permute-start(bf16[56,512]{1,0:T(8,128)(2,1)S(1)} %add_convert_fusion.1), channel_id=1, source_target_pairs={{0,3},{1,0},{2,1},{3,2},{4,7},{5,4},{6,5},{7,6},{8,11},{9,8},{10,9... | collective-permute-start | bytes 172040 | tf_op jit(solution)/shard_map/ppermute | solution.py:189
  158.3 2.5 %collective-permute-done.9 = bf16[56,512]{1,0:T(8,128)(2,1)S(1)} collective-permute-done((bf16[56,512]{1,0:T(8,128)(2,1)S(1)}, bf16[56,512]{1,0:T(8,128)(2,1)S(1)}, u32[]{:S(2)}, u32[]{:S(2)}) %collective-permute-start.9) | collective-permute-done | bytes 57376 | tf_op jit(solution)/shard_map/ppermute | solution.py:188
  160.8 15.2 %collective-permute-done.11 = bf16[56,512]{1,0:T(8,128)(2,1)S(1)} collective-permute-done((bf16[56,512]{1,0:T(8,128)(2,1)S(1)}, bf16[56,512]{1,0:T(8,128)(2,1)S(1)}, u32[]{:S(2)}, u32[]{:S(2)}) %collective-permute-start.11) | collective-permute-done | bytes 57376 | tf_op jit(solution)/shard_map/ppermute | solution.py:189
  176.1 0.1 add_convert_fusion.2
  176.1 0.1 concatenate.22
  176.2 0.1 concatenate.21
  176.4 0.1 copy.6
  176.5 0.2 reshape.30
  176.7 13.2 %all_to_all.15 = bf16[16,2,1792]{2,1,0:T(2,128)(2,1)S(1)} all-to-all(bf16[16,2,1792]{2,1,0:T(2,128)(2,1)S(1)} %reshape.30), channel_id=1, replica_groups=mesh['expert'=16,'y'=4,'x'=4,'micro'=4] {'y','x'}, dimensions={0} | all-to-all | bytes 229376 | tf_op jit(solution)/shard_map/all_to_all | solution.py:230
  189.8 0.2 reshape.31
  190.1 0.9 copy.8
  (19 shorter events, 0.3 us)
Async XLA Ops:
  0.0 1.2 copy-start.1
  1.2 0.7 copy-start.3
  1.8 0.7 copy-start.4
  4.3 12.8 %copy-start.2 = (bf16[160,1024]{1,0:T(8,128)(2,1)S(1)}, bf16[160,1024]{1,0:T(8,128)(2,1)}, u32[]{:S(2)}) copy-start(bf16[160,1024]{1,0:T(8,128)(2,1)} %hidden_ref.1) | copy-start | bytes 983044
  4.3 60.3 %all-to-all-start = ((bf16[16,8,4480]{2,1,0:T(8,128)(2,1)}), bf16[16,8,4480]{2,1,0:T(8,128)(2,1)S(1)}, u32[]{:S(2)}, u32[]{:S(2)}) async-start(bf16[16,8,4480]{2,1,0:T(8,128)(2,1)} %bitcast.4), calls=%async_computation | async-start | bytes 2293760 | tf_op jit(solution)/shard_map/all_to_all | solution.py:220
  17.3 13.6 %collective-permute-start = (bf16[160,1024]{1,0:T(8,128)(2,1)S(1)}, bf16[160,1024]{1,0:T(8,128)(2,1)S(1)}, u32[]{:S(2)}, u32[]{:S(2)}) collective-permute-start(bf16[160,1024]{1,0:T(8,128)(2,1)S(1)} %order.1), channel_id=1, source_target_pairs={{0,12},{4,0},{8,4},{12,8},{1,13},{5,1},{9,5},{13,9},{2,14},{6,2},{... | collective-permute-start | bytes 983048 | tf_op jit(solution)/shard_map/ppermute | solution.py:201
  23.5 11.8 %collective-permute-start.1 = (bf16[160,1024]{1,0:T(8,128)(2,1)S(1)}, bf16[160,1024]{1,0:T(8,128)(2,1)S(1)}, u32[]{:S(2)}, u32[]{:S(2)}) collective-permute-start(bf16[160,1024]{1,0:T(8,128)(2,1)S(1)} %order.1), channel_id=1, source_target_pairs={{0,4},{4,8},{8,12},{12,0},{1,5},{5,9},{9,13},{13,1},{2,6},{6,10},{... | collective-permute-start | bytes 983048 | tf_op jit(solution)/shard_map/ppermute | solution.py:200
  30.9 7.5 %collective-permute-start.3 = (bf16[80,1024]{1,0:T(8,128)(2,1)S(1)}, bf16[80,1024]{1,0:T(8,128)(2,1)S(1)}, u32[]{:S(2)}, u32[]{:S(2)}) collective-permute-start(bf16[80,1024]{1,0:T(8,128)(2,1)S(1)} %slice.65), channel_id=1, source_target_pairs={{0,12},{4,0},{8,4},{12,8},{1,13},{5,1},{9,5},{13,9},{2,14},{6,2},{... | collective-permute-start | bytes 491528 | tf_op jit(solution)/shard_map/ppermute | solution.py:203
  35.3 7.3 %collective-permute-start.2 = (bf16[80,1024]{1,0:T(8,128)(2,1)S(1)}, bf16[80,1024]{1,0:T(8,128)(2,1)S(1)}, u32[]{:S(2)}, u32[]{:S(2)}) collective-permute-start(bf16[80,1024]{1,0:T(8,128)(2,1)S(1)} %slice.64), channel_id=1, source_target_pairs={{0,4},{4,8},{8,12},{12,0},{1,5},{5,9},{9,13},{13,1},{2,6},{6,10},{... | collective-permute-start | bytes 491528 | tf_op jit(solution)/shard_map/ppermute | solution.py:202
  42.8 32.3 %collective-permute-start.5 = (bf16[4,160,1024]{2,1,0:T(8,128)(2,1)S(1)}, bf16[4,160,1024]{2,1,0:T(8,128)(2,1)}, u32[]{:S(2)}, u32[]{:S(2)}) collective-permute-start(bf16[4,160,1024]{2,1,0:T(8,128)(2,1)S(1)} %pad_maximum_fusion.refs_0_), channel_id=1, source_target_pairs={{0,16},{16,32},{32,48},{48,0},{1,17},{17,33},{33,49},{49,1},{2,18}... | collective-permute-start | bytes 3932168 | tf_op jit(solution)/shard_map/ppermute | solution.py:200
  45.0 36.5 %collective-permute-start.4 = (bf16[4,160,1024]{2,1,0:T(8,128)(2,1)S(1)}, bf16[4,160,1024]{2,1,0:T(8,128)(2,1)}, u32[]{:S(2)}, u32[]{:S(2)}) collective-permute-start(bf16[4,160,1024]{2,1,0:T(8,128)(2,1)S(1)} %pad_maximum_fusion.refs_0_), channel_id=1, source_target_pairs={{0,48},{16,0},{32,16},{48,32},{1,49},{17,1},{33,17},{49,33},{2,50}... | collective-permute-start | bytes 3932168 | tf_op jit(solution)/shard_map/ppermute | solution.py:201
  64.9 1.0 copy-start
  65.9 38.5 %all-to-all-start.1 = ((bf16[16,280,128]{2,1,0:T(8,128)(2,1)}), bf16[16,280,128]{2,1,0:T(8,128)(2,1)S(1)}, u32[]{:S(2)}, u32[]{:S(2)}) async-start(bf16[16,280,128]{2,1,0:T(8,128)(2,1)} %copy-done), calls=%async_computation.1 | async-start | bytes 2293760 | tf_op jit(solution)/shard_map/all_to_all | solution.py:224
  77.0 27.4 %collective-permute-start.6 = (bf16[4,80,1024]{2,1,0:T(8,128)(2,1)}, bf16[4,80,1024]{2,1,0:T(8,128)(2,1)S(1)}, u32[]{:S(2)}, u32[]{:S(2)}) collective-permute-start(bf16[4,80,1024]{2,1,0:T(8,128)(2,1)} %slice.66), channel_id=1, source_target_pairs={{0,16},{16,32},{32,48},{48,0},{1,17},{17,33},{33,49},{49,1},{2,18}... | collective-permute-start | bytes 1966088 | tf_op jit(solution)/shard_map/ppermute | solution.py:202
  83.5 20.9 %collective-permute-start.7 = (bf16[4,80,1024]{2,1,0:T(8,128)(2,1)}, bf16[4,80,1024]{2,1,0:T(8,128)(2,1)}, u32[]{:S(2)}, u32[]{:S(2)}) collective-permute-start(bf16[4,80,1024]{2,1,0:T(8,128)(2,1)} %slice.67), channel_id=1, source_target_pairs={{0,48},{16,0},{32,16},{48,32},{1,49},{17,1},{33,17},{49,33},{2,50}... | collective-permute-start | bytes 1966088 | tf_op jit(solution)/shard_map/ppermute | solution.py:203
  108.5 34.4 %collective-permute-start.8 = (bf16[56,1024]{1,0:T(8,128)(2,1)S(1)}, bf16[56,1024]{1,0:T(8,128)(2,1)S(1)}, u32[]{:S(2)}, u32[]{:S(2)}) collective-permute-start(bf16[56,1024]{1,0:T(8,128)(2,1)S(1)} %pad_maximum_fusion.1), channel_id=1, source_target_pairs={{0,1},{1,2},{2,3},{3,0},{4,5},{5,6},{6,7},{7,4},{8,9},{9,10},{10,1... | collective-permute-start | bytes 344072 | tf_op jit(solution)/shard_map/ppermute | solution.py:184
  123.7 32.7 %collective-permute-start.10 = (bf16[56,1024]{1,0:T(8,128)(2,1)S(1)}, bf16[56,1024]{1,0:T(8,128)(2,1)S(1)}, u32[]{:S(2)}, u32[]{:S(2)}) collective-permute-start(bf16[56,1024]{1,0:T(8,128)(2,1)S(1)} %pad_maximum_fusion.2), channel_id=1, source_target_pairs={{0,3},{1,0},{2,1},{3,2},{4,7},{5,4},{6,5},{7,6},{8,11},{9,8},{10,9... | collective-permute-start | bytes 344072 | tf_op jit(solution)/shard_map/ppermute | solution.py:185
  142.9 17.9 %collective-permute-start.9 = (bf16[56,512]{1,0:T(8,128)(2,1)S(1)}, bf16[56,512]{1,0:T(8,128)(2,1)S(1)}, u32[]{:S(2)}, u32[]{:S(2)}) collective-permute-start(bf16[56,512]{1,0:T(8,128)(2,1)S(1)} %add_convert_fusion.3), channel_id=1, source_target_pairs={{0,1},{1,2},{2,3},{3,0},{4,5},{5,6},{6,7},{7,4},{8,9},{9,10},{10,1... | collective-permute-start | bytes 172040 | tf_op jit(solution)/shard_map/ppermute | solution.py:188
  156.4 19.7 %collective-permute-start.11 = (bf16[56,512]{1,0:T(8,128)(2,1)S(1)}, bf16[56,512]{1,0:T(8,128)(2,1)S(1)}, u32[]{:S(2)}, u32[]{:S(2)}) collective-permute-start(bf16[56,512]{1,0:T(8,128)(2,1)S(1)} %add_convert_fusion.1), channel_id=1, source_target_pairs={{0,3},{1,0},{2,1},{3,2},{4,7},{5,4},{6,5},{7,6},{8,11},{9,8},{10,9... | collective-permute-start | bytes 172040 | tf_op jit(solution)/shard_map/ppermute | solution.py:189

commit v3 on v2

--- a/solution.py
+++ b/solution.py
@@ -10,6 +10,7 @@
 
 FIRST = 8
 VMEM = 48 * 1024 * 1024
+WHOLE_VMEM = 60 * 1024 * 1024
 
 
 REPLICA = ("y", "x")
@@ -60,8 +61,9 @@
         ).astype(jnp.bfloat16)
 
 
-def order_kernel(capacity, hidden_ref, out_ref):
-    places = hidden_ref.shape[0]
+def order_kernel(capacity, *refs):
+    own_ref, before_ref, low_ref, high_ref, behind_ref, out_ref = refs
+    places = own_ref.shape[0]
     extra = capacity - FIRST
     senders = places // capacity
     row, place = iota((places, places), 0), iota((places, places), 1)
@@ -72,12 +74,12 @@
         late // extra * capacity + FIRST + late % extra,
     )
     chosen = (source == place).astype(jnp.bfloat16)
-    out_ref[...] = jnp.dot(
-        chosen, hidden_ref[...], preferred_element_type=jnp.float32
-    ).astype(jnp.bfloat16)
-
-
-def product_kernel(parts, extra, spot_ref, moved_ref, *refs):
+    far = jnp.concatenate([low_ref[...], high_ref[...]], axis=0)
+    for i, block in enumerate((own_ref[...], before_ref[...], far, behind_ref[...])):
+        out_ref[i] = jnp.dot(chosen, block, preferred_element_type=jnp.float32).astype(jnp.bfloat16)
+
+
+def product_kernel(parts, extra, far, spot_ref, moved_ref, *refs):
     *hidden, out_ref = refs
     copies, rows, slots = moved_ref.shape
     side = hidden[0].shape[0]
@@ -95,8 +97,8 @@
         ).astype(jnp.bfloat16)
         for q in range(parts)
     ]
-    total = jnp.zeros(out_ref.shape, jnp.float32)
-    for k in range(side):
+    total = None
+    for k, *held in [(2, *hidden[:2])] if far else [(0, hidden[0]), (1, hidden[1]), (3, hidden[2])]:
         y = lax.rem(spot_ref[0] + k, side)
         moved = [moved_ref[y * side + lax.rem(spot_ref[1] + j, side)] for j in range(side)]
         behind = jnp.concatenate(
@@ -105,30 +107,30 @@
         late = [jnp.dot(behind, g, preferred_element_type=jnp.float32) for g in goes]
         left = [m[: parts * piece] for m in moved]
         left.append(jnp.concatenate(late, axis=0).astype(jnp.bfloat16))
-        if k == 2:
-            low, high = hidden[2], hidden[3]
-            cut = slots - low.shape[1]
-            first = [part for j in range(side) for part in (low[j], high[j][:cut])]
-            last = [high[j][cut:] for j in range(side)]
-        else:
-            held = hidden[k if k < 2 else k + 1]
-            first = [held[j][:slots] for j in range(side)]
-            last = [held[j][slots:] for j in range(side)]
-        total += jnp.dot(
+        first, last = [], []
+        for j in range(side):
+            *whole, end = [h[j] for h in held]
+            cut = slots - sum(w.shape[0] for w in whole)
+            first += [*whole, end[:cut]]
+            last.append(end[cut:])
+        product = jnp.dot(
             jnp.concatenate(left, axis=1),
             jnp.concatenate(first + last, axis=0),
             preferred_element_type=jnp.float32,
         )
-    out_ref[...] = total.astype(jnp.bfloat16)
-
-
-def order(hidden, capacity):
+        total = product if total is None else total + product
+    if far:
+        total += hidden[2][...]
+    out_ref[...] = total.astype(out_ref.dtype)
+
+
+def order(blocks, capacity):
     return pl.pallas_call(
         functools.partial(order_kernel, capacity),
-        out_shape=jax.ShapeDtypeStruct(hidden.shape, jnp.bfloat16),
+        out_shape=jax.ShapeDtypeStruct((4, *blocks[0].shape), jnp.bfloat16),
         compiler_params=pltpu.CompilerParams(vmem_limit_bytes=VMEM),
         name="order",
-    )(hidden)
+    )(*blocks)
 
 
 def dispatch(rows, target, weight, experts, capacity, parts):
@@ -137,7 +139,7 @@
     return pl.pallas_call(
         functools.partial(dispatch_kernel, capacity, parts),
         out_shape=jax.ShapeDtypeStruct(shape, jnp.bfloat16),
-        compiler_params=pltpu.CompilerParams(vmem_limit_bytes=VMEM),
+        compiler_params=pltpu.CompilerParams(vmem_limit_bytes=WHOLE_VMEM),
         name="dispatch",
     )(rows, target.reshape(1, tokens), weight.reshape(1, tokens))
 
@@ -157,14 +159,20 @@
     features = hidden[0].shape[2]
     out = (rows // (parts + 1) * parts, features)
     inside = pl.BlockSpec(memory_space=pltpu.VMEM)
-    return pl.pallas_call(
-        functools.partial(product_kernel, parts, capacity - FIRST),
-        in_specs=[pl.BlockSpec(memory_space=pltpu.SMEM)] + [inside] * (1 + len(hidden)),
-        out_specs=inside,
-        out_shape=jax.ShapeDtypeStruct(out, jnp.bfloat16),
-        compiler_params=pltpu.CompilerParams(vmem_limit_bytes=VMEM),
-        name="product",
-    )(spot, moved, *hidden)
+
+    def call(far, blocks, kind):
+        return pl.pallas_call(
+            functools.partial(product_kernel, parts, capacity - FIRST, far),
+            in_specs=[pl.BlockSpec(memory_space=pltpu.SMEM)] + [inside] * (1 + len(blocks)),
+            out_specs=inside,
+            out_shape=jax.ShapeDtypeStruct(out, kind),
+            compiler_params=pltpu.CompilerParams(vmem_limit_bytes=VMEM),
+            name="far_product" if far else "near_product",
+        )(spot, moved, *blocks)
+
+    own, before, low, high, behind = hidden
+    near = call(False, (own, before, behind), jnp.float32)
+    return call(True, (low, high, near), jnp.bfloat16)
 
 
 def sum_over_micro(partial):
@@ -204,19 +212,16 @@
     return block, before, low, high, behind
 
 
-def gather_hidden(block):
-    own, before, low, high, behind = ring_gather(block, "x")
-    row = jnp.stack([own, before, jnp.concatenate([low, high], axis=0), behind])
-    return ring_gather(row, "y")
+def gather_hidden(block, capacity):
+    return ring_gather(order(ring_gather(block, "x"), capacity), "y")
 
 
 def shards(grad_rows, routing, route_weight, saved_hidden):
     experts, copies, parts = (lax.axis_size(a) for a in ("expert", REPLICA, "micro"))
     places, features = saved_hidden.shape
     capacity = places // experts
-    hidden = order(saved_hidden, capacity)
     sent = dispatch(grad_rows, routing, route_weight, experts, capacity, parts)
-    hidden = gather_hidden(hidden)
+    hidden = gather_hidden(saved_hidden, capacity)
     arrived = lax.all_to_all(
         sent.reshape(experts, FIRST, -1), "expert", split_axis=0, concat_axis=0, tiled=True
     )

time: 192 us -> 190 us (0.990)
  the two profiles are of different devices: /device:TPU:2 before, /device:TPU:32 now
where the time goes in v3:
time: 190 us; the launch traced here: 189 us
  starting transfers between devices  80.3 us (42%)
  waiting for transfers between devices  78.9 us (42%)
  blocking collectives  12.1 us (6%)
  Pallas kernels  10.2 us (5%)
  local copies, waits for them, and re-layouts  6.58 us (3%)
    all_to_all x1, waiting for transfers between devices, shards(): lax.all_to_all(sent.reshape(experts, FIRST, -1), 'expert', split_axis=0,...  20.9 us
    ppermute x1, waiting for transfers between devices, sum_over_micro(): lax.ppermute(jnp.concatenate([left[:, :half], far[:, half:]], 1), 'micro'...  18.2 us
    all_to_all x1, starting transfers between devices, shards(): lax.all_to_all(sent.reshape(experts, FIRST, -1), 'expert', split_axis=0,...  17 us
    ppermute x1, starting transfers between devices, sum_over_micro(): lax.ppermute(jnp.concatenate([left[:, :half], far[:, half:]], 1), 'micro'...  14.5 us
    all_to_all x1, blocking collectives, shards(): out = lax.all_to_all(out, REPLICA, split_axis=0, concat_axis=0, tiled=True)  12.1 us
    all_to_all x1, waiting for transfers between devices, shards(): lax.all_to_all(turned, REPLICA, split_axis=0, concat_axis=0, tiled=True)  11.2 us
    ppermute x2, starting transfers between devices, ring_gather(): before = lax.ppermute(block, axis, back)  10.3 us
    ppermute x1, starting transfers between devices, sum_over_micro(): down_late = lax.ppermute(down_late, 'micro', back)  9.77 us
  transfers between devices with their start and end apart: 14, of which 9 were waited for; matrix products, arithmetic and copies ran while one was open for 2% of the time, Pallas kernels for 3%

profile of v3, /device:TPU:32, one launch (start us, length us, event | category | flops | bytes accessed | tf_op | source)
XLA Modules:
  0.0 188.7 jit_solution(1103609894505805961)
XLA Ops:
  0.0 3.0 %dispatch.1 = bf16[128,4480]{1,0:T(8,128)(2,1)} custom-call(bf16[128,3584]{1,0:T(8,128)(2,1)} %rows_ref.1, s32[1,128]{1,0:T(1,128)} %bitcast.25, f32[1,128]{1,0:T(1,128)} %bitcast.26), custom_call_target="tpu_custom_call" | custom-call | tf_op jit(solution)/shard_map/dispatch/pallas_call | solution.py:139
  3.0 0.0 copy-start.1
  3.0 17.0 %all-to-all-start = ((bf16[16,8,4480]{2,1,0:T(8,128)(2,1)}), bf16[16,8,4480]{2,1,0:T(8,128)(2,1)}, u32[]{:S(2)}, u32[]{:S(2)}) async-start(bf16[16,8,4480]{2,1,0:T(8,128)(2,1)} %bitcast.24), calls=%async_computation | async-start | bytes 2293760 | tf_op jit(solution)/shard_map/all_to_all | solution.py:225
  20.0 0.0 copy-done.1
  20.0 1.9 %collective-permute-start.1 = (bf16[160,1024]{1,0:T(8,128)(2,1)S(1)}, bf16[160,1024]{1,0:T(8,128)(2,1)S(1)}, u32[]{:S(2)}, u32[]{:S(2)}) collective-permute-start(bf16[160,1024]{1,0:T(8,128)(2,1)S(1)} %copy-done.1), channel_id=1, source_target_pairs={{0,4},{4,8},{8,12},{12,0},{1,5},{5,9},{9,13},{13,1},{2,6},{6,10},{... | collective-permute-start | bytes 983048 | tf_op jit(solution)/shard_map/ppermute | solution.py:208
  21.9 5.1 %collective-permute-start = (bf16[160,1024]{1,0:T(8,128)(2,1)S(1)}, bf16[160,1024]{1,0:T(8,128)(2,1)S(1)}, u32[]{:S(2)}, u32[]{:S(2)}) collective-permute-start(bf16[160,1024]{1,0:T(8,128)(2,1)S(1)} %copy-done.1), channel_id=1, source_target_pairs={{0,12},{4,0},{8,4},{12,8},{1,13},{5,1},{9,5},{13,9},{2,14},{6,2},{... | collective-permute-start | bytes 983048 | tf_op jit(solution)/shard_map/ppermute | solution.py:209
  27.1 5.8 %collective-permute-done.1.refs_4_ = bf16[160,1024]{1,0:T(8,128)(2,1)S(1)} collective-permute-done((bf16[160,1024]{1,0:T(8,128)(2,1)S(1)}, bf16[160,1024]{1,0:T(8,128)(2,1)S(1)}, u32[]{:S(2)}, u32[]{:S(2)}) %collective-permute-start.1) | collective-permute-done | bytes 327712 | tf_op jit(solution)/shard_map/ppermute | solution.py:208
  32.9 1.9 %collective-permute-start.2 = (bf16[80,1024]{1,0:T(8,128)(2,1)S(1)}, bf16[80,1024]{1,0:T(8,128)(2,1)S(1)}, u32[]{:S(2)}, u32[]{:S(2)}) collective-permute-start(bf16[80,1024]{1,0:T(8,128)(2,1)S(1)} %slice.64), channel_id=1, source_target_pairs={{0,4},{4,8},{8,12},{12,0},{1,5},{5,9},{9,13},{13,1},{2,6},{6,10},{... | collective-permute-start | bytes 491528 | tf_op jit(solution)/shard_map/ppermute | solution.py:210
  34.8 0.0 collective-permute-done.refs_1_
  34.8 5.1 %collective-permute-start.3 = (bf16[80,1024]{1,0:T(8,128)(2,1)S(1)}, bf16[80,1024]{1,0:T(8,128)(2,1)S(1)}, u32[]{:S(2)}, u32[]{:S(2)}) collective-permute-start(bf16[80,1024]{1,0:T(8,128)(2,1)S(1)} %slice.65), channel_id=1, source_target_pairs={{0,12},{4,0},{8,4},{12,8},{1,13},{5,1},{9,5},{13,9},{2,14},{6,2},{... | collective-permute-start | bytes 491528 | tf_op jit(solution)/shard_map/ppermute | solution.py:211
  40.0 1.4 collective-permute-done.2.refs_2_
  41.4 1.4 collective-permute-done.3.refs_3_
  42.8 0.5 order.1.refs_0_
  43.3 1.9 %collective-permute-start.4 = (bf16[4,160,1024]{2,1,0:T(8,128)(2,1)S(1)}, bf16[4,160,1024]{2,1,0:T(8,128)(2,1)}, u32[]{:S(2)}, u32[]{:S(2)}) collective-permute-start(bf16[4,160,1024]{2,1,0:T(8,128)(2,1)S(1)} %order.1.refs_0_), channel_id=1, source_target_pairs={{0,16},{16,32},{32,48},{48,0},{1,17},{17,33},{33,49},{49,1},{2,18}... | collective-permute-start | bytes 3932168 | tf_op jit(solution)/shard_map/ppermute | solution.py:208
  45.2 5.1 %collective-permute-start.6 = (bf16[4,160,1024]{2,1,0:T(8,128)(2,1)S(1)}, bf16[4,160,1024]{2,1,0:T(8,128)(2,1)}, u32[]{:S(2)}, u32[]{:S(2)}) collective-permute-start(bf16[4,160,1024]{2,1,0:T(8,128)(2,1)S(1)} %order.1.refs_0_), channel_id=1, source_target_pairs={{0,48},{16,0},{32,16},{48,32},{1,49},{17,1},{33,17},{49,33},{2,50}... | collective-permute-start | bytes 3932168 | tf_op jit(solution)/shard_map/ppermute | solution.py:209
  50.3 20.9 %all-to-all-done = bf16[16,8,4480]{2,1,0:T(8,128)(2,1)} async-done(((bf16[16,8,4480]{2,1,0:T(8,128)(2,1)}), bf16[16,8,4480]{2,1,0:T(8,128)(2,1)}, u32[]{:S(2)}, u32[]{:S(2)}) %all-to-all-start) | async-done | bytes 1146912 | tf_op jit(solution)/shard_map/all_to_all | solution.py:225
  71.2 1.6 turn.1
  72.9 0.0 copy-start
  72.9 1.0 copy-done
  73.9 3.7 %all-to-all-start.1 = ((bf16[16,280,128]{2,1,0:T(8,128)(2,1)}), bf16[16,280,128]{2,1,0:T(8,128)(2,1)S(1)}, u32[]{:S(2)}, u32[]{:S(2)}) async-start(bf16[16,280,128]{2,1,0:T(8,128)(2,1)} %copy-done), calls=%async_computation.1 | async-start | bytes 2293760 | tf_op jit(solution)/shard_map/all_to_all | solution.py:229
  77.6 0.0 collective-permute-done.4.refs_2_
  77.6 2.0 %slice.66 = bf16[4,80,1024]{2,1,0:T(8,128)(2,1)} slice(bf16[4,160,1024]{2,1,0:T(8,128)(2,1)} %collective-permute-done.4.refs_2_), slice={[0:4], [0:80], [0:1024]} | slice | bytes 1310720 | tf_op jit(solution)/shard_map/slice | solution.py:210
  79.6 3.7 %collective-permute-start.5 = (bf16[4,80,1024]{2,1,0:T(8,128)(2,1)}, bf16[4,80,1024]{2,1,0:T(8,128)(2,1)S(1)}, u32[]{:S(2)}, u32[]{:S(2)}) collective-permute-start(bf16[4,80,1024]{2,1,0:T(8,128)(2,1)} %slice.66), channel_id=1, source_target_pairs={{0,16},{16,32},{32,48},{48,0},{1,17},{17,33},{33,49},{49,1},{2,18}... | collective-permute-start | bytes 1966088 | tf_op jit(solution)/shard_map/ppermute | solution.py:210
  83.3 0.0 collective-permute-done.6.refs_1_
  83.3 2.0 %slice.67 = bf16[4,80,1024]{2,1,0:T(8,128)(2,1)} slice(bf16[4,160,1024]{2,1,0:T(8,128)(2,1)} %collective-permute-done.6.refs_1_), slice={[0:4], [80:160], [0:1024]} | slice | bytes 1310720 | tf_op jit(solution)/shard_map/slice | solution.py:211
  85.3 3.3 %collective-permute-start.7 = (bf16[4,80,1024]{2,1,0:T(8,128)(2,1)}, bf16[4,80,1024]{2,1,0:T(8,128)(2,1)}, u32[]{:S(2)}, u32[]{:S(2)}) collective-permute-start(bf16[4,80,1024]{2,1,0:T(8,128)(2,1)} %slice.67), channel_id=1, source_target_pairs={{0,48},{16,0},{32,16},{48,32},{1,49},{17,1},{33,17},{49,33},{2,50}... | collective-permute-start | bytes 1966088 | tf_op jit(solution)/shard_map/ppermute | solution.py:211
  88.7 0.1 pad_add_fusion.spot_ref
  88.7 11.2 %all-to-all-done.1.moved_ref = bf16[16,280,128]{2,1,0:T(8,128)(2,1)S(1)} async-done(((bf16[16,280,128]{2,1,0:T(8,128)(2,1)}), bf16[16,280,128]{2,1,0:T(8,128)(2,1)S(1)}, u32[]{:S(2)}, u32[]{:S(2)}) %all-to-all-start.1) | async-done | bytes 1146912 | tf_op jit(solution)/shard_map/all_to_all | solution.py:229
  99.9 3.3 %near_product.1.refs_2_ = f32[224,1024]{1,0:T(8,128)S(1)} custom-call(s32[2]{0:T(128)S(1)} %pad_add_fusion.spot_ref, bf16[16,280,128]{2,1,0:T(8,128)(2,1)S(1)} %all-to-all-done.1.moved_ref, bf16[4,160,1024]{2,1,0:T(8,128)(2,1)S(1)} %order.1.refs_0_, bf16[4,160,1024]{2,1,0:T(8,128)(2,1)} %collective-permute-done.6.refs_1_, ...), custom_call_target="tpu_custom_call" | custom-call | tf_op jit(solution)/shard_map/near_product/pallas_call | solution.py:164
  103.3 5.8 %collective-permute-done.5.refs_0_ = bf16[4,80,1024]{2,1,0:T(8,128)(2,1)S(1)} collective-permute-done((bf16[4,80,1024]{2,1,0:T(8,128)(2,1)}, bf16[4,80,1024]{2,1,0:T(8,128)(2,1)S(1)}, u32[]{:S(2)}, u32[]{:S(2)}) %collective-permute-start.5) | collective-permute-done | bytes 655392 | tf_op jit(solution)/shard_map/ppermute | solution.py:210
  109.0 0.0 collective-permute-done.7.refs_1_
  109.0 1.8 far_product.1
  110.9 14.5 %collective-permute-start.10 = (bf16[56,1024]{1,0:T(8,128)(2,1)S(1)}, bf16[56,1024]{1,0:T(8,128)(2,1)S(1)}, u32[]{:S(2)}, u32[]{:S(2)}) collective-permute-start(bf16[56,1024]{1,0:T(8,128)(2,1)S(1)} %pad_maximum_fusion.1), channel_id=1, source_target_pairs={{0,3},{1,0},{2,1},{3,2},{4,7},{5,4},{6,5},{7,6},{8,11},{9,8},{10,9... | collective-permute-start | bytes 344072 | tf_op jit(solution)/shard_map/ppermute | solution.py:193
  125.4 2.1 %collective-permute-start.8 = (bf16[56,1024]{1,0:T(8,128)(2,1)S(1)}, bf16[56,1024]{1,0:T(8,128)(2,1)S(1)}, u32[]{:S(2)}, u32[]{:S(2)}) collective-permute-start(bf16[56,1024]{1,0:T(8,128)(2,1)S(1)} %pad_maximum_fusion), channel_id=1, source_target_pairs={{0,1},{1,2},{2,3},{3,0},{4,5},{5,6},{6,7},{7,4},{8,9},{9,10},{10,1... | collective-permute-start | bytes 344072 | tf_op jit(solution)/shard_map/ppermute | solution.py:192
  127.6 18.2 %collective-permute-done.10 = bf16[56,1024]{1,0:T(8,128)(2,1)S(1)} collective-permute-done((bf16[56,1024]{1,0:T(8,128)(2,1)S(1)}, bf16[56,1024]{1,0:T(8,128)(2,1)S(1)}, u32[]{:S(2)}, u32[]{:S(2)}) %collective-permute-start.10) | collective-permute-done | bytes 114720 | tf_op jit(solution)/shard_map/ppermute | solution.py:193
  145.8 9.8 %collective-permute-start.11 = (bf16[56,512]{1,0:T(8,128)(2,1)S(1)}, bf16[56,512]{1,0:T(8,128)(2,1)S(1)}, u32[]{:S(2)}, u32[]{:S(2)}) collective-permute-start(bf16[56,512]{1,0:T(8,128)(2,1)S(1)} %add_convert_fusion.1), channel_id=1, source_target_pairs={{0,3},{1,0},{2,1},{3,2},{4,7},{5,4},{6,5},{7,6},{8,11},{9,8},{10,9... | collective-permute-start | bytes 172040 | tf_op jit(solution)/shard_map/ppermute | solution.py:197
  155.6 0.0 collective-permute-done.8
  155.6 5.0 %collective-permute-start.9 = (bf16[56,512]{1,0:T(8,128)(2,1)S(1)}, bf16[56,512]{1,0:T(8,128)(2,1)S(1)}, u32[]{:S(2)}, u32[]{:S(2)}) collective-permute-start(bf16[56,512]{1,0:T(8,128)(2,1)S(1)} %add_convert_fusion.3), channel_id=1, source_target_pairs={{0,1},{1,2},{2,3},{3,0},{4,5},{5,6},{6,7},{7,4},{8,9},{9,10},{10,1... | collective-permute-start | bytes 172040 | tf_op jit(solution)/shard_map/ppermute | solution.py:196
  160.6 4.5 %collective-permute-done.11 = bf16[56,512]{1,0:T(8,128)(2,1)S(1)} collective-permute-done((bf16[56,512]{1,0:T(8,128)(2,1)S(1)}, bf16[56,512]{1,0:T(8,128)(2,1)S(1)}, u32[]{:S(2)}, u32[]{:S(2)}) %collective-permute-start.11) | collective-permute-done | bytes 57376 | tf_op jit(solution)/shard_map/ppermute | solution.py:197
  165.2 9.7 %collective-permute-done.9 = bf16[56,512]{1,0:T(8,128)(2,1)S(1)} collective-permute-done((bf16[56,512]{1,0:T(8,128)(2,1)S(1)}, bf16[56,512]{1,0:T(8,128)(2,1)S(1)}, u32[]{:S(2)}, u32[]{:S(2)}) %collective-permute-start.9) | collective-permute-done | bytes 57376 | tf_op jit(solution)/shard_map/ppermute | solution.py:196
  174.9 0.1 add_convert_fusion.2
  174.9 0.1 concatenate.17
  175.1 0.1 concatenate.18
  175.3 0.1 copy.6
  175.3 0.2 reshape.30
  175.5 12.1 %all_to_all.15 = bf16[16,2,1792]{2,1,0:T(2,128)(2,1)S(1)} all-to-all(bf16[16,2,1792]{2,1,0:T(2,128)(2,1)S(1)} %reshape.30), channel_id=1, replica_groups=mesh['expert'=16,'y'=4,'x'=4,'micro'=4] {'y','x'}, dimensions={0} | all-to-all | bytes 229376 | tf_op jit(solution)/shard_map/all_to_all | solution.py:235
  187.6 0.2 reshape.31
  187.9 0.9 copy.8
  (12 shorter events, 0.2 us)
Async XLA Ops:
  3.0 17.0 %copy-start.1 = (bf16[160,1024]{1,0:T(8,128)(2,1)S(1)}, bf16[160,1024]{1,0:T(8,128)(2,1)}, u32[]{:S(2)}) copy-start(bf16[160,1024]{1,0:T(8,128)(2,1)} %refs_0_.1) | copy-start | bytes 983044
  3.0 68.3 %all-to-all-start = ((bf16[16,8,4480]{2,1,0:T(8,128)(2,1)}), bf16[16,8,4480]{2,1,0:T(8,128)(2,1)}, u32[]{:S(2)}, u32[]{:S(2)}) async-start(bf16[16,8,4480]{2,1,0:T(8,128)(2,1)} %bitcast.24), calls=%async_computation | async-start | bytes 2293760 | tf_op jit(solution)/shard_map/all_to_all | solution.py:225
  20.0 12.9 %collective-permute-start.1 = (bf16[160,1024]{1,0:T(8,128)(2,1)S(1)}, bf16[160,1024]{1,0:T(8,128)(2,1)S(1)}, u32[]{:S(2)}, u32[]{:S(2)}) collective-permute-start(bf16[160,1024]{1,0:T(8,128)(2,1)S(1)} %copy-done.1), channel_id=1, source_target_pairs={{0,4},{4,8},{8,12},{12,0},{1,5},{5,9},{9,13},{13,1},{2,6},{6,10},{... | collective-permute-start | bytes 983048 | tf_op jit(solution)/shard_map/ppermute | solution.py:208
  21.9 12.9 %collective-permute-start = (bf16[160,1024]{1,0:T(8,128)(2,1)S(1)}, bf16[160,1024]{1,0:T(8,128)(2,1)S(1)}, u32[]{:S(2)}, u32[]{:S(2)}) collective-permute-start(bf16[160,1024]{1,0:T(8,128)(2,1)S(1)} %copy-done.1), channel_id=1, source_target_pairs={{0,12},{4,0},{8,4},{12,8},{1,13},{5,1},{9,5},{13,9},{2,14},{6,2},{... | collective-permute-start | bytes 983048 | tf_op jit(solution)/shard_map/ppermute | solution.py:209
  32.9 8.5 %collective-permute-start.2 = (bf16[80,1024]{1,0:T(8,128)(2,1)S(1)}, bf16[80,1024]{1,0:T(8,128)(2,1)S(1)}, u32[]{:S(2)}, u32[]{:S(2)}) collective-permute-start(bf16[80,1024]{1,0:T(8,128)(2,1)S(1)} %slice.64), channel_id=1, source_target_pairs={{0,4},{4,8},{8,12},{12,0},{1,5},{5,9},{9,13},{13,1},{2,6},{6,10},{... | collective-permute-start | bytes 491528 | tf_op jit(solution)/shard_map/ppermute | solution.py:210
  34.8 8.0 %collective-permute-start.3 = (bf16[80,1024]{1,0:T(8,128)(2,1)S(1)}, bf16[80,1024]{1,0:T(8,128)(2,1)S(1)}, u32[]{:S(2)}, u32[]{:S(2)}) collective-permute-start(bf16[80,1024]{1,0:T(8,128)(2,1)S(1)} %slice.65), channel_id=1, source_target_pairs={{0,12},{4,0},{8,4},{12,8},{1,13},{5,1},{9,5},{13,9},{2,14},{6,2},{... | collective-permute-start | bytes 491528 | tf_op jit(solution)/shard_map/ppermute | solution.py:211
  43.3 34.3 %collective-permute-start.4 = (bf16[4,160,1024]{2,1,0:T(8,128)(2,1)S(1)}, bf16[4,160,1024]{2,1,0:T(8,128)(2,1)}, u32[]{:S(2)}, u32[]{:S(2)}) collective-permute-start(bf16[4,160,1024]{2,1,0:T(8,128)(2,1)S(1)} %order.1.refs_0_), channel_id=1, source_target_pairs={{0,16},{16,32},{32,48},{48,0},{1,17},{17,33},{33,49},{49,1},{2,18}... | collective-permute-start | bytes 3932168 | tf_op jit(solution)/shard_map/ppermute | solution.py:208
  45.2 38.1 %collective-permute-start.6 = (bf16[4,160,1024]{2,1,0:T(8,128)(2,1)S(1)}, bf16[4,160,1024]{2,1,0:T(8,128)(2,1)}, u32[]{:S(2)}, u32[]{:S(2)}) collective-permute-start(bf16[4,160,1024]{2,1,0:T(8,128)(2,1)S(1)} %order.1.refs_0_), channel_id=1, source_target_pairs={{0,48},{16,0},{32,16},{48,32},{1,49},{17,1},{33,17},{49,33},{2,50}... | collective-permute-start | bytes 3932168 | tf_op jit(solution)/shard_map/ppermute | solution.py:209
  72.9 1.0 copy-start
  73.9 26.1 %all-to-all-start.1 = ((bf16[16,280,128]{2,1,0:T(8,128)(2,1)}), bf16[16,280,128]{2,1,0:T(8,128)(2,1)S(1)}, u32[]{:S(2)}, u32[]{:S(2)}) async-start(bf16[16,280,128]{2,1,0:T(8,128)(2,1)} %copy-done), calls=%async_computation.1 | async-start | bytes 2293760 | tf_op jit(solution)/shard_map/all_to_all | solution.py:229
  79.6 29.4 %collective-permute-start.5 = (bf16[4,80,1024]{2,1,0:T(8,128)(2,1)}, bf16[4,80,1024]{2,1,0:T(8,128)(2,1)S(1)}, u32[]{:S(2)}, u32[]{:S(2)}) collective-permute-start(bf16[4,80,1024]{2,1,0:T(8,128)(2,1)} %slice.66), channel_id=1, source_target_pairs={{0,16},{16,32},{32,48},{48,0},{1,17},{17,33},{33,49},{49,1},{2,18}... | collective-permute-start | bytes 1966088 | tf_op jit(solution)/shard_map/ppermute | solution.py:210
  85.3 23.7 %collective-permute-start.7 = (bf16[4,80,1024]{2,1,0:T(8,128)(2,1)}, bf16[4,80,1024]{2,1,0:T(8,128)(2,1)}, u32[]{:S(2)}, u32[]{:S(2)}) collective-permute-start(bf16[4,80,1024]{2,1,0:T(8,128)(2,1)} %slice.67), channel_id=1, source_target_pairs={{0,48},{16,0},{32,16},{48,32},{1,49},{17,1},{33,17},{49,33},{2,50}... | collective-permute-start | bytes 1966088 | tf_op jit(solution)/shard_map/ppermute | solution.py:211
  110.9 34.9 %collective-permute-start.10 = (bf16[56,1024]{1,0:T(8,128)(2,1)S(1)}, bf16[56,1024]{1,0:T(8,128)(2,1)S(1)}, u32[]{:S(2)}, u32[]{:S(2)}) collective-permute-start(bf16[56,1024]{1,0:T(8,128)(2,1)S(1)} %pad_maximum_fusion.1), channel_id=1, source_target_pairs={{0,3},{1,0},{2,1},{3,2},{4,7},{5,4},{6,5},{7,6},{8,11},{9,8},{10,9... | collective-permute-start | bytes 344072 | tf_op jit(solution)/shard_map/ppermute | solution.py:193
  125.4 30.2 %collective-permute-start.8 = (bf16[56,1024]{1,0:T(8,128)(2,1)S(1)}, bf16[56,1024]{1,0:T(8,128)(2,1)S(1)}, u32[]{:S(2)}, u32[]{:S(2)}) collective-permute-start(bf16[56,1024]{1,0:T(8,128)(2,1)S(1)} %pad_maximum_fusion), channel_id=1, source_target_pairs={{0,1},{1,2},{2,3},{3,0},{4,5},{5,6},{6,7},{7,4},{8,9},{9,10},{10,1... | collective-permute-start | bytes 344072 | tf_op jit(solution)/shard_map/ppermute | solution.py:192
  145.8 19.4 %collective-permute-start.11 = (bf16[56,512]{1,0:T(8,128)(2,1)S(1)}, bf16[56,512]{1,0:T(8,128)(2,1)S(1)}, u32[]{:S(2)}, u32[]{:S(2)}) collective-permute-start(bf16[56,512]{1,0:T(8,128)(2,1)S(1)} %add_convert_fusion.1), channel_id=1, source_target_pairs={{0,3},{1,0},{2,1},{3,2},{4,7},{5,4},{6,5},{7,6},{8,11},{9,8},{10,9... | collective-permute-start | bytes 172040 | tf_op jit(solution)/shard_map/ppermute | solution.py:197
  155.6 19.3 %collective-permute-start.9 = (bf16[56,512]{1,0:T(8,128)(2,1)S(1)}, bf16[56,512]{1,0:T(8,128)(2,1)S(1)}, u32[]{:S(2)}, u32[]{:S(2)}) collective-permute-start(bf16[56,512]{1,0:T(8,128)(2,1)S(1)} %add_convert_fusion.3), channel_id=1, source_target_pairs={{0,1},{1,2},{2,3},{3,0},{4,5},{5,6},{6,7},{7,4},{8,9},{9,10},{10,1... | collective-permute-start | bytes 172040 | tf_op jit(solution)/shard_map/ppermute | solution.py:196

commit v4 on v3

--- a/solution.py
+++ b/solution.py
@@ -1,4 +1,5 @@
 import functools
+import math
 
 import jax
 import jax.numpy as jnp
@@ -62,8 +63,8 @@
 
 
 def order_kernel(capacity, *refs):
-    own_ref, before_ref, low_ref, high_ref, behind_ref, out_ref = refs
-    places = own_ref.shape[0]
+    *blocks, out_ref = refs
+    places = out_ref.shape[1]
     extra = capacity - FIRST
     senders = places // capacity
     row, place = iota((places, places), 0), iota((places, places), 1)
@@ -74,15 +75,16 @@
         late // extra * capacity + FIRST + late % extra,
     )
     chosen = (source == place).astype(jnp.bfloat16)
-    far = jnp.concatenate([low_ref[...], high_ref[...]], axis=0)
-    for i, block in enumerate((own_ref[...], before_ref[...], far, behind_ref[...])):
-        out_ref[i] = jnp.dot(chosen, block, preferred_element_type=jnp.float32).astype(jnp.bfloat16)
+    for i, block in enumerate(blocks):
+        out_ref[i] = jnp.dot(
+            chosen, block[...], preferred_element_type=jnp.float32
+        ).astype(jnp.bfloat16)
 
 
 def product_kernel(parts, extra, far, spot_ref, moved_ref, *refs):
     *hidden, out_ref = refs
     copies, rows, slots = moved_ref.shape
-    side = hidden[0].shape[0]
+    side = math.isqrt(copies)
     piece = rows // (parts + 1)
     senders = slots // FIRST
     lane, place = iota((slots, slots), 0), iota((slots, slots), 1)
@@ -98,21 +100,17 @@
         for q in range(parts)
     ]
     total = None
-    for k, *held in [(2, *hidden[:2])] if far else [(0, hidden[0]), (1, hidden[1]), (3, hidden[2])]:
-        y = lax.rem(spot_ref[0] + k, side)
-        moved = [moved_ref[y * side + lax.rem(spot_ref[1] + j, side)] for j in range(side)]
+    for k, held in [(2, hidden[0])] if far else [(0, hidden[0]), (1, hidden[1]), (3, hidden[2])]:
+        y = lax.rem(spot_ref[0] + k * spot_ref[2], side)
+        moved = [moved_ref[y * side + lax.rem(spot_ref[1] + j * spot_ref[2], side)] for j in range(side)]
         behind = jnp.concatenate(
             [m[parts * piece :].astype(jnp.float32) for m in moved], axis=1
         ).astype(jnp.bfloat16)
         late = [jnp.dot(behind, g, preferred_element_type=jnp.float32) for g in goes]
         left = [m[: parts * piece] for m in moved]
         left.append(jnp.concatenate(late, axis=0).astype(jnp.bfloat16))
-        first, last = [], []
-        for j in range(side):
-            *whole, end = [h[j] for h in held]
-            cut = slots - sum(w.shape[0] for w in whole)
-            first += [*whole, end[:cut]]
-            last.append(end[cut:])
+        first = [held[j][:slots] for j in range(side)]
+        last = [held[j][slots:] for j in range(side)]
         product = jnp.dot(
             jnp.concatenate(left, axis=1),
             jnp.concatenate(first + last, axis=0),
@@ -120,7 +118,7 @@
         )
         total = product if total is None else total + product
     if far:
-        total += hidden[2][...]
+        total += hidden[1][...]
     out_ref[...] = total.astype(out_ref.dtype)
 
 
@@ -170,46 +168,46 @@
             name="far_product" if far else "near_product",
         )(spot, moved, *blocks)
 
-    own, before, low, high, behind = hidden
-    near = call(False, (own, before, behind), jnp.float32)
-    return call(True, (low, high, near), jnp.bfloat16)
+    own, one_back, two_back, three_back = hidden
+    near = call(False, (own, one_back, three_back), jnp.float32)
+    return call(True, (two_back, near), jnp.bfloat16)
+
+
+def way():
+    return 1 - 2 * (lax.axis_index("expert") % 2)
+
+
+def step(block, axis, steps):
+    size, experts = lax.axis_size(axis), lax.axis_size("expert")
+    perm = [
+        (e * size + i, e * size + (i + steps * (1 - 2 * (e % 2))) % size)
+        for e in range(experts)
+        for i in range(size)
+    ]
+    return lax.ppermute(block, ("expert", axis), perm)
 
 
 def sum_over_micro(partial):
-    size = 4
-    me = lax.axis_index("micro")
-    half = partial.shape[2] // 2
-    ahead = [(i, (i + 1) % size) for i in range(size)]
-    back = [(i, (i - 1) % size) for i in range(size)]
-
-    def part(k):
-        return lax.dynamic_index_in_dim(partial, (me + k) % size, 0, keepdims=False)
+    me, size = lax.axis_index("micro"), lax.axis_size("micro")
+
+    def part(steps):
+        place = (me + way() * steps + size) % size
+        return lax.dynamic_index_in_dim(partial, place, 0, keepdims=False)
 
     def wide(v):
         return v.astype(jnp.float32)
 
-    own, right, far, left = (part(k) for k in range(size))
-    up = lax.ppermute(jnp.concatenate([far[:, :half], right[:, half:]], 1), "micro", ahead)
-    down = lax.ppermute(jnp.concatenate([left[:, :half], far[:, half:]], 1), "micro", back)
-    up_late = (wide(right[:, :half]) + wide(up[:, :half])).astype(partial.dtype)
-    down_late = (wide(left[:, half:]) + wide(down[:, half:])).astype(partial.dtype)
-    up_late = lax.ppermute(up_late, "micro", ahead)
-    down_late = lax.ppermute(down_late, "micro", back)
-    low = wide(own[:, :half]) + wide(up_late) + wide(down[:, :half])
-    high = wide(own[:, half:]) + wide(up[:, half:]) + wide(down_late)
-    return jnp.concatenate([low, high], 1).astype(partial.dtype)
+    came = step(part(2), "micro", 1)
+    direct = step(part(-1), "micro", -1)
+    late = step((wide(part(1)) + wide(came)).astype(partial.dtype), "micro", 1)
+    return (wide(part(0)) + wide(direct) + wide(late)).astype(partial.dtype)
 
 
 def ring_gather(block, axis):
-    size = lax.axis_size(axis)
-    ahead = [(i, (i + 1) % size) for i in range(size)]
-    back = [(i, (i - 1) % size) for i in range(size)]
-    half = block.shape[-2] // 2
-    behind = lax.ppermute(block, axis, ahead)
-    before = lax.ppermute(block, axis, back)
-    low = lax.ppermute(behind[..., :half, :], axis, ahead)
-    high = lax.ppermute(before[..., half:, :], axis, back)
-    return block, before, low, high, behind
+    one_back = step(block, axis, 1)
+    three_back = step(block, axis, -1)
+    two_back = step(one_back, axis, 1)
+    return block, one_back, two_back, three_back
 
 
 def gather_hidden(block, capacity):
@@ -227,7 +225,7 @@
     )
     turned = turn(arrived.reshape(experts * FIRST, -1), copies, parts)
     moved = lax.all_to_all(turned, REPLICA, split_axis=0, concat_axis=0, tiled=True)
-    spot = jnp.stack([lax.axis_index("y"), lax.axis_index("x")])
+    spot = jnp.stack([lax.axis_index("y"), lax.axis_index("x"), 4 - way()])
     partial = product(moved, hidden, spot, capacity, parts)
     part = sum_over_micro(partial.reshape(parts, -1, features))
     piece = part.shape[0]

time: 190 us -> 177 us (0.932)
  the two profiles are of different devices: /device:TPU:32 before, /device:TPU:2 now
where the time goes in v4:
time: 177 us
  waiting for transfers between devices  72.9 us (41%)
  starting transfers between devices  70.6 us (40%)
  blocking collectives  21.1 us (12%)
  Pallas kernels  9.12 us (5%)
  local copies, waits for them, and re-layouts  2.51 us (1%)
    ppermute x9, waiting for transfers between devices, step(): return lax.ppermute(block, ('expert', axis), perm)  53.3 us
    ppermute x9, starting transfers between devices, step(): return lax.ppermute(block, ('expert', axis), perm)  48.3 us
    all_to_all x1, blocking collectives, shards(): out = lax.all_to_all(out, REPLICA, split_axis=0, concat_axis=0, tiled=True)  21.1 us
    all_to_all x1, waiting for transfers between devices, shards(): lax.all_to_all(turned, REPLICA, split_axis=0, concat_axis=0, tiled=True)  19.6 us
    all_to_all x1, starting transfers between devices, shards(): lax.all_to_all(sent.reshape(experts, FIRST, -1), 'expert', split_axis=0,...  12.8 us
    all_to_all x1, starting transfers between devices, shards(): lax.all_to_all(turned, REPLICA, split_axis=0, concat_axis=0, tiled=True)  9.61 us
    pallas_call x2, Pallas kernels, call(): pl.pallas_call(functools.partial(product_kernel, parts, capacity - FIRST,...  5.3 us
  transfers between devices with their start and end apart: 11, of which 7 were waited for; matrix products, arithmetic and copies ran while one was open for 0% of the time, Pallas kernels for 2%

profile of v4, /device:TPU:2, one launch (start us, length us, event | category | flops | bytes accessed | tf_op | source)
XLA Modules:
  0.0 176.7 jit_solution(1502993884658492903)
XLA Ops:
  0.0 3.0 %dispatch.1 = bf16[128,4480]{1,0:T(8,128)(2,1)} custom-call(bf16[128,3584]{1,0:T(8,128)(2,1)} %rows_ref.1, s32[1,128]{1,0:T(1,128)} %bitcast.31, f32[1,128]{1,0:T(1,128)} %bitcast.32), custom_call_target="tpu_custom_call" | custom-call | tf_op jit(solution)/shard_map/dispatch/pallas_call | solution.py:137
  3.0 0.0 copy-start.1
  3.0 12.8 %all-to-all-start = ((bf16[16,8,4480]{2,1,0:T(8,128)(2,1)}), bf16[16,8,4480]{2,1,0:T(8,128)(2,1)S(1)}, u32[]{:S(2)}, u32[]{:S(2)}) async-start(bf16[16,8,4480]{2,1,0:T(8,128)(2,1)} %bitcast.29), calls=%async_computation | async-start | bytes 2293760 | tf_op jit(solution)/shard_map/all_to_all | solution.py:223
  15.7 0.0 copy-done.1
  15.8 3.4 %collective-permute-start = (bf16[160,1024]{1,0:T(8,128)(2,1)S(1)}, bf16[160,1024]{1,0:T(8,128)(2,1)S(1)}, u32[]{:S(2)}, u32[]{:S(2)}) collective-permute-start(bf16[160,1024]{1,0:T(8,128)(2,1)S(1)} %copy-done.1), channel_id=1, source_target_pairs={{0,4},{4,8},{8,12},{12,0},{64,76},{68,64},{72,68},{76,72},{128,132... | collective-permute-start | bytes 983048 | tf_op jit(solution)/shard_map/ppermute | solution.py:187
  19.2 4.7 %collective-permute-start.2 = (bf16[160,1024]{1,0:T(8,128)(2,1)S(1)}, bf16[160,1024]{1,0:T(8,128)(2,1)S(1)}, u32[]{:S(2)}, u32[]{:S(2)}) collective-permute-start(bf16[160,1024]{1,0:T(8,128)(2,1)S(1)} %copy-done.1), channel_id=1, source_target_pairs={{0,12},{4,0},{8,4},{12,8},{64,68},{68,72},{72,76},{76,64},{128,140... | collective-permute-start | bytes 983048 | tf_op jit(solution)/shard_map/ppermute | solution.py:187
  23.8 3.6 %collective-permute-done.refs_1_ = bf16[160,1024]{1,0:T(8,128)(2,1)S(1)} collective-permute-done((bf16[160,1024]{1,0:T(8,128)(2,1)S(1)}, bf16[160,1024]{1,0:T(8,128)(2,1)S(1)}, u32[]{:S(2)}, u32[]{:S(2)}) %collective-permute-start) | collective-permute-done | bytes 327712 | tf_op jit(solution)/shard_map/ppermute | solution.py:187
  27.4 1.9 %collective-permute-start.1 = (bf16[160,1024]{1,0:T(8,128)(2,1)S(1)}, bf16[160,1024]{1,0:T(8,128)(2,1)S(1)}, u32[]{:S(2)}, u32[]{:S(2)}) collective-permute-start(bf16[160,1024]{1,0:T(8,128)(2,1)S(1)} %collective-permute-done.refs_1_), channel_id=1, source_target_pairs={{0,4},{4,8},{8,12},{12,0},{64,76},{68,64},{72,68},{76,72},{128,132... | collective-permute-start | bytes 983048 | tf_op jit(solution)/shard_map/ppermute | solution.py:187
  29.4 0.0 collective-permute-done.2.refs_3_
  29.4 10.0 %collective-permute-done.1.refs_2_ = bf16[160,1024]{1,0:T(8,128)(2,1)S(1)} collective-permute-done((bf16[160,1024]{1,0:T(8,128)(2,1)S(1)}, bf16[160,1024]{1,0:T(8,128)(2,1)S(1)}, u32[]{:S(2)}, u32[]{:S(2)}) %collective-permute-start.1) | collective-permute-done | bytes 327712 | tf_op jit(solution)/shard_map/ppermute | solution.py:187
  39.4 0.5 order.1.refs_0_
  39.9 1.9 %collective-permute-start.3 = (bf16[4,160,1024]{2,1,0:T(8,128)(2,1)S(1)}, bf16[4,160,1024]{2,1,0:T(8,128)(2,1)}, u32[]{:S(2)}, u32[]{:S(2)}) collective-permute-start(bf16[4,160,1024]{2,1,0:T(8,128)(2,1)S(1)} %order.1.refs_0_), channel_id=1, source_target_pairs={{0,16},{16,32},{32,48},{48,0},{64,112},{80,64},{96,80},{112,96},{1... | collective-permute-start | bytes 3932168 | tf_op jit(solution)/shard_map/ppermute | solution.py:187
  41.8 5.1 %collective-permute-start.5 = (bf16[4,160,1024]{2,1,0:T(8,128)(2,1)S(1)}, bf16[4,160,1024]{2,1,0:T(8,128)(2,1)}, u32[]{:S(2)}, u32[]{:S(2)}) collective-permute-start(bf16[4,160,1024]{2,1,0:T(8,128)(2,1)S(1)} %order.1.refs_0_), channel_id=1, source_target_pairs={{0,48},{16,0},{32,16},{48,32},{64,80},{80,96},{96,112},{112,64},{1... | collective-permute-start | bytes 3932168 | tf_op jit(solution)/shard_map/ppermute | solution.py:187
  46.9 24.5 %collective-permute-done.3.refs_1_ = bf16[4,160,1024]{2,1,0:T(8,128)(2,1)} collective-permute-done((bf16[4,160,1024]{2,1,0:T(8,128)(2,1)S(1)}, bf16[4,160,1024]{2,1,0:T(8,128)(2,1)}, u32[]{:S(2)}, u32[]{:S(2)}) %collective-permute-start.3) | collective-permute-done | bytes 1310752 | tf_op jit(solution)/shard_map/ppermute | solution.py:187
  71.4 2.2 %collective-permute-start.4 = (bf16[4,160,1024]{2,1,0:T(8,128)(2,1)}, bf16[4,160,1024]{2,1,0:T(8,128)(2,1)}, u32[]{:S(2)}, u32[]{:S(2)}) collective-permute-start(bf16[4,160,1024]{2,1,0:T(8,128)(2,1)} %collective-permute-done.3.refs_1_), channel_id=1, source_target_pairs={{0,16},{16,32},{32,48},{48,0},{64,112},{80,64},{96,80},{112,96},{1... | collective-permute-start | bytes 3932168 | tf_op jit(solution)/shard_map/ppermute | solution.py:187
  73.6 0.0 all-to-all-done
  73.6 0.4 turn.1
  74.0 0.0 copy-start
  74.0 1.0 copy-done
  75.0 9.6 %all-to-all-start.1 = ((bf16[16,280,128]{2,1,0:T(8,128)(2,1)}), bf16[16,280,128]{2,1,0:T(8,128)(2,1)S(1)}, u32[]{:S(2)}, u32[]{:S(2)}) async-start(bf16[16,280,128]{2,1,0:T(8,128)(2,1)} %copy-done), calls=%async_computation.1 | async-start | bytes 2293760 | tf_op jit(solution)/shard_map/all_to_all | solution.py:227
  84.6 0.1 pad_add_fusion.spot_ref
  84.7 0.0 collective-permute-done.5.refs_2_
  84.7 19.6 %all-to-all-done.1.moved_ref = bf16[16,280,128]{2,1,0:T(8,128)(2,1)S(1)} async-done(((bf16[16,280,128]{2,1,0:T(8,128)(2,1)}), bf16[16,280,128]{2,1,0:T(8,128)(2,1)S(1)}, u32[]{:S(2)}, u32[]{:S(2)}) %all-to-all-start.1) | async-done | bytes 1146912 | tf_op jit(solution)/shard_map/all_to_all | solution.py:227
  104.3 3.3 %near_product.1.refs_1_ = f32[224,1024]{1,0:T(8,128)S(1)} custom-call(s32[3]{0:T(128)S(1)} %pad_add_fusion.spot_ref, bf16[16,280,128]{2,1,0:T(8,128)(2,1)S(1)} %all-to-all-done.1.moved_ref, bf16[4,160,1024]{2,1,0:T(8,128)(2,1)S(1)} %order.1.refs_0_, bf16[4,160,1024]{2,1,0:T(8,128)(2,1)} %collective-permute-done.3.refs_1_, ...), custom_call_target="tpu_custom_call" | custom-call | tf_op jit(solution)/shard_map/near_product/pallas_call | solution.py:162
  107.6 0.0 collective-permute-done.4.refs_0_
  107.6 2.0 %far_product.1 = bf16[224,1024]{1,0:T(8,128)(2,1)S(1)} custom-call(s32[3]{0:T(128)S(1)} %pad_add_fusion.spot_ref, bf16[16,280,128]{2,1,0:T(8,128)(2,1)S(1)} %all-to-all-done.1.moved_ref, bf16[4,160,1024]{2,1,0:T(8,128)(2,1)} %collective-permute-done.4.refs_0_, f32[224,1024]{1,0:T(8,128)S(1)} %near_product.1.refs_1_), custom_call_target="tpu_custom_call" | custom-call | tf_op jit(solution)/shard_map/far_product/pallas_call | solution.py:162
  109.6 13.8 %collective-permute-start.7 = (bf16[56,1024]{1,0:T(8,128)(2,1)S(1)}, bf16[56,1024]{1,0:T(8,128)(2,1)S(1)}, u32[]{:S(2)}, u32[]{:S(2)}) collective-permute-start(bf16[56,1024]{1,0:T(8,128)(2,1)S(1)} %get-tuple-element.6), channel_id=1, source_target_pairs={{0,1},{1,2},{2,3},{3,0},{64,67},{65,64},{66,65},{67,66},{128,129},... | collective-permute-start | bytes 344072 | tf_op jit(solution)/shard_map/ppermute | solution.py:187
  123.5 1.9 %collective-permute-start.6 = (bf16[56,1024]{1,0:T(8,128)(2,1)S(1)}, bf16[56,1024]{1,0:T(8,128)(2,1)S(1)}, u32[]{:S(2)}, u32[]{:S(2)}) collective-permute-start(bf16[56,1024]{1,0:T(8,128)(2,1)S(1)} %get-tuple-element.5), channel_id=1, source_target_pairs={{0,3},{1,0},{2,1},{3,2},{64,65},{65,66},{66,67},{67,64},{128,131},... | collective-permute-start | bytes 344072 | tf_op jit(solution)/shard_map/ppermute | solution.py:187
  125.4 2.0 %collective-permute-done.7 = bf16[56,1024]{1,0:T(8,128)(2,1)S(1)} collective-permute-done((bf16[56,1024]{1,0:T(8,128)(2,1)S(1)}, bf16[56,1024]{1,0:T(8,128)(2,1)S(1)}, u32[]{:S(2)}, u32[]{:S(2)}) %collective-permute-start.7) | collective-permute-done | bytes 114720 | tf_op jit(solution)/shard_map/ppermute | solution.py:187
  127.4 13.3 %collective-permute-start.8 = (bf16[56,1024]{1,0:T(8,128)(2,1)S(1)}, bf16[56,1024]{1,0:T(8,128)(2,1)S(1)}, u32[]{:S(2)}, u32[]{:S(2)}) collective-permute-start(bf16[56,1024]{1,0:T(8,128)(2,1)S(1)} %fusion), channel_id=1, source_target_pairs={{0,1},{1,2},{2,3},{3,0},{64,67},{65,64},{66,65},{67,66},{128,129},... | collective-permute-start | bytes 344072 | tf_op jit(solution)/shard_map/ppermute | solution.py:187
  140.8 4.0 %collective-permute-done.6 = bf16[56,1024]{1,0:T(8,128)(2,1)S(1)} collective-permute-done((bf16[56,1024]{1,0:T(8,128)(2,1)S(1)}, bf16[56,1024]{1,0:T(8,128)(2,1)S(1)}, u32[]{:S(2)}, u32[]{:S(2)}) %collective-permute-start.6) | collective-permute-done | bytes 114720 | tf_op jit(solution)/shard_map/ppermute | solution.py:187
  144.7 9.3 %collective-permute-done.8 = bf16[56,1024]{1,0:T(8,128)(2,1)S(1)} collective-permute-done((bf16[56,1024]{1,0:T(8,128)(2,1)S(1)}, bf16[56,1024]{1,0:T(8,128)(2,1)S(1)}, u32[]{:S(2)}, u32[]{:S(2)}) %collective-permute-start.8) | collective-permute-done | bytes 114720 | tf_op jit(solution)/shard_map/ppermute | solution.py:187
  154.1 0.2 reshape.30
  154.3 0.1 copy.7
  154.3 0.2 reshape.35
  154.5 21.1 %all_to_all.15 = bf16[16,2,1792]{2,1,0:T(2,128)(2,1)S(1)} all-to-all(bf16[16,2,1792]{2,1,0:T(2,128)(2,1)S(1)} %reshape.35), channel_id=1, replica_groups=mesh['expert'=16,'y'=4,'x'=4,'micro'=4] {'y','x'}, dimensions={0} | all-to-all | bytes 229376 | tf_op jit(solution)/shard_map/all_to_all | solution.py:233
  175.6 0.2 reshape.36
  175.8 0.9 copy.9
  (4 shorter events, 0.2 us)
Async XLA Ops:
  3.0 12.8 %copy-start.1 = (bf16[160,1024]{1,0:T(8,128)(2,1)S(1)}, bf16[160,1024]{1,0:T(8,128)(2,1)}, u32[]{:S(2)}) copy-start(bf16[160,1024]{1,0:T(8,128)(2,1)} %refs_0_.1) | copy-start | bytes 983044
  3.0 70.6 %all-to-all-start = ((bf16[16,8,4480]{2,1,0:T(8,128)(2,1)}), bf16[16,8,4480]{2,1,0:T(8,128)(2,1)S(1)}, u32[]{:S(2)}, u32[]{:S(2)}) async-start(bf16[16,8,4480]{2,1,0:T(8,128)(2,1)} %bitcast.29), calls=%async_computation | async-start | bytes 2293760 | tf_op jit(solution)/shard_map/all_to_all | solution.py:223
  15.8 11.7 %collective-permute-start = (bf16[160,1024]{1,0:T(8,128)(2,1)S(1)}, bf16[160,1024]{1,0:T(8,128)(2,1)S(1)}, u32[]{:S(2)}, u32[]{:S(2)}) collective-permute-start(bf16[160,1024]{1,0:T(8,128)(2,1)S(1)} %copy-done.1), channel_id=1, source_target_pairs={{0,4},{4,8},{8,12},{12,0},{64,76},{68,64},{72,68},{76,72},{128,132... | collective-permute-start | bytes 983048 | tf_op jit(solution)/shard_map/ppermute | solution.py:187
  19.2 10.2 %collective-permute-start.2 = (bf16[160,1024]{1,0:T(8,128)(2,1)S(1)}, bf16[160,1024]{1,0:T(8,128)(2,1)S(1)}, u32[]{:S(2)}, u32[]{:S(2)}) collective-permute-start(bf16[160,1024]{1,0:T(8,128)(2,1)S(1)} %copy-done.1), channel_id=1, source_target_pairs={{0,12},{4,0},{8,4},{12,8},{64,68},{68,72},{72,76},{76,64},{128,140... | collective-permute-start | bytes 983048 | tf_op jit(solution)/shard_map/ppermute | solution.py:187
  27.4 11.9 %collective-permute-start.1 = (bf16[160,1024]{1,0:T(8,128)(2,1)S(1)}, bf16[160,1024]{1,0:T(8,128)(2,1)S(1)}, u32[]{:S(2)}, u32[]{:S(2)}) collective-permute-start(bf16[160,1024]{1,0:T(8,128)(2,1)S(1)} %collective-permute-done.refs_1_), channel_id=1, source_target_pairs={{0,4},{4,8},{8,12},{12,0},{64,76},{68,64},{72,68},{76,72},{128,132... | collective-permute-start | bytes 983048 | tf_op jit(solution)/shard_map/ppermute | solution.py:187
  39.9 31.6 %collective-permute-start.3 = (bf16[4,160,1024]{2,1,0:T(8,128)(2,1)S(1)}, bf16[4,160,1024]{2,1,0:T(8,128)(2,1)}, u32[]{:S(2)}, u32[]{:S(2)}) collective-permute-start(bf16[4,160,1024]{2,1,0:T(8,128)(2,1)S(1)} %order.1.refs_0_), channel_id=1, source_target_pairs={{0,16},{16,32},{32,48},{48,0},{64,112},{80,64},{96,80},{112,96},{1... | collective-permute-start | bytes 3932168 | tf_op jit(solution)/shard_map/ppermute | solution.py:187
  41.8 42.9 %collective-permute-start.5 = (bf16[4,160,1024]{2,1,0:T(8,128)(2,1)S(1)}, bf16[4,160,1024]{2,1,0:T(8,128)(2,1)}, u32[]{:S(2)}, u32[]{:S(2)}) collective-permute-start(bf16[4,160,1024]{2,1,0:T(8,128)(2,1)S(1)} %order.1.refs_0_), channel_id=1, source_target_pairs={{0,48},{16,0},{32,16},{48,32},{64,80},{80,96},{96,112},{112,64},{1... | collective-permute-start | bytes 3932168 | tf_op jit(solution)/shard_map/ppermute | solution.py:187
  71.4 36.2 %collective-permute-start.4 = (bf16[4,160,1024]{2,1,0:T(8,128)(2,1)}, bf16[4,160,1024]{2,1,0:T(8,128)(2,1)}, u32[]{:S(2)}, u32[]{:S(2)}) collective-permute-start(bf16[4,160,1024]{2,1,0:T(8,128)(2,1)} %collective-permute-done.3.refs_1_), channel_id=1, source_target_pairs={{0,16},{16,32},{32,48},{48,0},{64,112},{80,64},{96,80},{112,96},{1... | collective-permute-start | bytes 3932168 | tf_op jit(solution)/shard_map/ppermute | solution.py:187
  74.0 1.0 copy-start
  75.0 29.3 %all-to-all-start.1 = ((bf16[16,280,128]{2,1,0:T(8,128)(2,1)}), bf16[16,280,128]{2,1,0:T(8,128)(2,1)S(1)}, u32[]{:S(2)}, u32[]{:S(2)}) async-start(bf16[16,280,128]{2,1,0:T(8,128)(2,1)} %copy-done), calls=%async_computation.1 | async-start | bytes 2293760 | tf_op jit(solution)/shard_map/all_to_all | solution.py:227
  109.6 17.8 %collective-permute-start.7 = (bf16[56,1024]{1,0:T(8,128)(2,1)S(1)}, bf16[56,1024]{1,0:T(8,128)(2,1)S(1)}, u32[]{:S(2)}, u32[]{:S(2)}) collective-permute-start(bf16[56,1024]{1,0:T(8,128)(2,1)S(1)} %get-tuple-element.6), channel_id=1, source_target_pairs={{0,1},{1,2},{2,3},{3,0},{64,67},{65,64},{66,65},{67,66},{128,129},... | collective-permute-start | bytes 344072 | tf_op jit(solution)/shard_map/ppermute | solution.py:187
  123.5 21.2 %collective-permute-start.6 = (bf16[56,1024]{1,0:T(8,128)(2,1)S(1)}, bf16[56,1024]{1,0:T(8,128)(2,1)S(1)}, u32[]{:S(2)}, u32[]{:S(2)}) collective-permute-start(bf16[56,1024]{1,0:T(8,128)(2,1)S(1)} %get-tuple-element.5), channel_id=1, source_target_pairs={{0,3},{1,0},{2,1},{3,2},{64,65},{65,66},{66,67},{67,64},{128,131},... | collective-permute-start | bytes 344072 | tf_op jit(solution)/shard_map/ppermute | solution.py:187
  127.4 26.6 %collective-permute-start.8 = (bf16[56,1024]{1,0:T(8,128)(2,1)S(1)}, bf16[56,1024]{1,0:T(8,128)(2,1)S(1)}, u32[]{:S(2)}, u32[]{:S(2)}) collective-permute-start(bf16[56,1024]{1,0:T(8,128)(2,1)S(1)} %fusion), channel_id=1, source_target_pairs={{0,1},{1,2},{2,3},{3,0},{64,67},{65,64},{66,65},{67,66},{128,129},... | collective-permute-start | bytes 344072 | tf_op jit(solution)/shard_map/ppermute | solution.py:187

commit v5 on v4

--- a/solution.py
+++ b/solution.py
@@ -81,7 +81,7 @@
         ).astype(jnp.bfloat16)
 
 
-def product_kernel(parts, extra, far, spot_ref, moved_ref, *refs):
+def product_kernel(parts, extra, spot_ref, moved_ref, *refs):
     *hidden, out_ref = refs
     copies, rows, slots = moved_ref.shape
     side = math.isqrt(copies)
@@ -100,7 +100,7 @@
         for q in range(parts)
     ]
     total = None
-    for k, held in [(2, hidden[0])] if far else [(0, hidden[0]), (1, hidden[1]), (3, hidden[2])]:
+    for k, held in enumerate(hidden):
         y = lax.rem(spot_ref[0] + k * spot_ref[2], side)
         moved = [moved_ref[y * side + lax.rem(spot_ref[1] + j * spot_ref[2], side)] for j in range(side)]
         behind = jnp.concatenate(
@@ -117,8 +117,6 @@
             preferred_element_type=jnp.float32,
         )
         total = product if total is None else total + product
-    if far:
-        total += hidden[1][...]
     out_ref[...] = total.astype(out_ref.dtype)
 
 
@@ -158,19 +156,14 @@
     out = (rows // (parts + 1) * parts, features)
     inside = pl.BlockSpec(memory_space=pltpu.VMEM)
 
-    def call(far, blocks, kind):
-        return pl.pallas_call(
-            functools.partial(product_kernel, parts, capacity - FIRST, far),
-            in_specs=[pl.BlockSpec(memory_space=pltpu.SMEM)] + [inside] * (1 + len(blocks)),
-            out_specs=inside,
-            out_shape=jax.ShapeDtypeStruct(out, kind),
-            compiler_params=pltpu.CompilerParams(vmem_limit_bytes=VMEM),
-            name="far_product" if far else "near_product",
-        )(spot, moved, *blocks)
-
-    own, one_back, two_back, three_back = hidden
-    near = call(False, (own, one_back, three_back), jnp.float32)
-    return call(True, (two_back, near), jnp.bfloat16)
+    return pl.pallas_call(
+        functools.partial(product_kernel, parts, capacity - FIRST),
+        in_specs=[pl.BlockSpec(memory_space=pltpu.SMEM)] + [inside] * (1 + len(hidden)),
+        out_specs=inside,
+        out_shape=jax.ShapeDtypeStruct(out, jnp.bfloat16),
+        compiler_params=pltpu.CompilerParams(vmem_limit_bytes=VMEM),
+        name="product",
+    )(spot, moved, *hidden)
 
 
 def way():

time: 177 us -> 176 us (level)
    all_to_all x1, waiting for transfers between devices: 19.6 us -> 0.66 us  [shards(): lax.all_to_all(turned, REPLICA, split_axis=0, concat_axis=0, tiled=True)]
    ppermute x9, waiting for transfers between devices: 53.3 us -> 72.2 us  [step(): return lax.ppermute(block, ('expert', axis), perm)]
    pallas_call x2 -> x1, Pallas kernels: 5.3 us -> 4.15 us  [product(): pl.pallas_call(functools.partial(product_kernel, parts, capacity - FIRST)...]
  transfers between devices with their start and end apart: 11 -> 11, of which waited for: 7 -> 8; matrix products, arithmetic and copies ran while one was open for 0% -> 0% of each run, Pallas kernels for 2% -> 0%
where the time goes in v5:
time: 176 us
  waiting for transfers between devices  72.9 us (41%)
  starting transfers between devices  70.6 us (40%)
  blocking collectives  21.1 us (12%)
  Pallas kernels  7.98 us (5%)
  local copies, waits for them, and re-layouts  2.51 us (1%)
    ppermute x9, waiting for transfers between devices, step(): return lax.ppermute(block, ('expert', axis), perm)  72.2 us
    ppermute x9, starting transfers between devices, step(): return lax.ppermute(block, ('expert', axis), perm)  48.3 us
    all_to_all x1, blocking collectives, shards(): out = lax.all_to_all(out, REPLICA, split_axis=0, concat_axis=0, tiled=True)  21.1 us
    all_to_all x1, starting transfers between devices, shards(): lax.all_to_all(sent.reshape(experts, FIRST, -1), 'expert', split_axis=0,...  12.8 us
    all_to_all x1, starting transfers between devices, shards(): lax.all_to_all(turned, REPLICA, split_axis=0, concat_axis=0, tiled=True)  9.61 us
    pallas_call x1, Pallas kernels, product(): pl.pallas_call(functools.partial(product_kernel, parts, capacity - FIRST)...  4.15 us
  transfers between devices with their start and end apart: 11, of which 8 were waited for; matrix products, arithmetic and copies ran while one was open for 0% of the time, Pallas kernels for 0%

profile of v5, /device:TPU:2, one launch (start us, length us, event | category | flops | bytes accessed | tf_op | source)
XLA Modules:
  0.0 175.5 jit_solution(15017603107187015994)
XLA Ops:
  0.0 3.0 %dispatch.1 = bf16[128,4480]{1,0:T(8,128)(2,1)} custom-call(bf16[128,3584]{1,0:T(8,128)(2,1)} %rows_ref.1, s32[1,128]{1,0:T(1,128)} %bitcast.31, f32[1,128]{1,0:T(1,128)} %bitcast.32), custom_call_target="tpu_custom_call" | custom-call | tf_op jit(solution)/shard_map/dispatch/pallas_call | solution.py:135
  3.0 0.0 copy-start.1
  3.0 12.8 %all-to-all-start = ((bf16[16,8,4480]{2,1,0:T(8,128)(2,1)}), bf16[16,8,4480]{2,1,0:T(8,128)(2,1)S(1)}, u32[]{:S(2)}, u32[]{:S(2)}) async-start(bf16[16,8,4480]{2,1,0:T(8,128)(2,1)} %bitcast.29), calls=%async_computation | async-start | bytes 2293760 | tf_op jit(solution)/shard_map/all_to_all | solution.py:216
  15.7 0.0 copy-done.1
  15.8 3.4 %collective-permute-start = (bf16[160,1024]{1,0:T(8,128)(2,1)S(1)}, bf16[160,1024]{1,0:T(8,128)(2,1)S(1)}, u32[]{:S(2)}, u32[]{:S(2)}) collective-permute-start(bf16[160,1024]{1,0:T(8,128)(2,1)S(1)} %copy-done.1), channel_id=1, source_target_pairs={{0,4},{4,8},{8,12},{12,0},{64,76},{68,64},{72,68},{76,72},{128,132... | collective-permute-start | bytes 983048 | tf_op jit(solution)/shard_map/ppermute | solution.py:180
  19.2 4.7 %collective-permute-start.2 = (bf16[160,1024]{1,0:T(8,128)(2,1)S(1)}, bf16[160,1024]{1,0:T(8,128)(2,1)S(1)}, u32[]{:S(2)}, u32[]{:S(2)}) collective-permute-start(bf16[160,1024]{1,0:T(8,128)(2,1)S(1)} %copy-done.1), channel_id=1, source_target_pairs={{0,12},{4,0},{8,4},{12,8},{64,68},{68,72},{72,76},{76,64},{128,140... | collective-permute-start | bytes 983048 | tf_op jit(solution)/shard_map/ppermute | solution.py:180
  23.8 3.6 %collective-permute-done.refs_1_ = bf16[160,1024]{1,0:T(8,128)(2,1)S(1)} collective-permute-done((bf16[160,1024]{1,0:T(8,128)(2,1)S(1)}, bf16[160,1024]{1,0:T(8,128)(2,1)S(1)}, u32[]{:S(2)}, u32[]{:S(2)}) %collective-permute-start) | collective-permute-done | bytes 327712 | tf_op jit(solution)/shard_map/ppermute | solution.py:180
  27.4 1.9 %collective-permute-start.1 = (bf16[160,1024]{1,0:T(8,128)(2,1)S(1)}, bf16[160,1024]{1,0:T(8,128)(2,1)S(1)}, u32[]{:S(2)}, u32[]{:S(2)}) collective-permute-start(bf16[160,1024]{1,0:T(8,128)(2,1)S(1)} %collective-permute-done.refs_1_), channel_id=1, source_target_pairs={{0,4},{4,8},{8,12},{12,0},{64,76},{68,64},{72,68},{76,72},{128,132... | collective-permute-start | bytes 983048 | tf_op jit(solution)/shard_map/ppermute | solution.py:180
  29.4 0.0 collective-permute-done.2.refs_3_
  29.4 10.0 %collective-permute-done.1.refs_2_ = bf16[160,1024]{1,0:T(8,128)(2,1)S(1)} collective-permute-done((bf16[160,1024]{1,0:T(8,128)(2,1)S(1)}, bf16[160,1024]{1,0:T(8,128)(2,1)S(1)}, u32[]{:S(2)}, u32[]{:S(2)}) %collective-permute-start.1) | collective-permute-done | bytes 327712 | tf_op jit(solution)/shard_map/ppermute | solution.py:180
  39.4 0.5 order.1.refs_0_
  39.9 1.9 %collective-permute-start.3 = (bf16[4,160,1024]{2,1,0:T(8,128)(2,1)S(1)}, bf16[4,160,1024]{2,1,0:T(8,128)(2,1)}, u32[]{:S(2)}, u32[]{:S(2)}) collective-permute-start(bf16[4,160,1024]{2,1,0:T(8,128)(2,1)S(1)} %order.1.refs_0_), channel_id=1, source_target_pairs={{0,16},{16,32},{32,48},{48,0},{64,112},{80,64},{96,80},{112,96},{1... | collective-permute-start | bytes 3932168 | tf_op jit(solution)/shard_map/ppermute | solution.py:180
  41.8 5.1 %collective-permute-start.5 = (bf16[4,160,1024]{2,1,0:T(8,128)(2,1)S(1)}, bf16[4,160,1024]{2,1,0:T(8,128)(2,1)}, u32[]{:S(2)}, u32[]{:S(2)}) collective-permute-start(bf16[4,160,1024]{2,1,0:T(8,128)(2,1)S(1)} %order.1.refs_0_), channel_id=1, source_target_pairs={{0,48},{16,0},{32,16},{48,32},{64,80},{80,96},{96,112},{112,64},{1... | collective-permute-start | bytes 3932168 | tf_op jit(solution)/shard_map/ppermute | solution.py:180
  46.9 24.5 %collective-permute-done.3.refs_1_ = bf16[4,160,1024]{2,1,0:T(8,128)(2,1)} collective-permute-done((bf16[4,160,1024]{2,1,0:T(8,128)(2,1)S(1)}, bf16[4,160,1024]{2,1,0:T(8,128)(2,1)}, u32[]{:S(2)}, u32[]{:S(2)}) %collective-permute-start.3) | collective-permute-done | bytes 1310752 | tf_op jit(solution)/shard_map/ppermute | solution.py:180
  71.4 2.2 %collective-permute-start.4 = (bf16[4,160,1024]{2,1,0:T(8,128)(2,1)}, bf16[4,160,1024]{2,1,0:T(8,128)(2,1)}, u32[]{:S(2)}, u32[]{:S(2)}) collective-permute-start(bf16[4,160,1024]{2,1,0:T(8,128)(2,1)} %collective-permute-done.3.refs_1_), channel_id=1, source_target_pairs={{0,16},{16,32},{32,48},{48,0},{64,112},{80,64},{96,80},{112,96},{1... | collective-permute-start | bytes 3932168 | tf_op jit(solution)/shard_map/ppermute | solution.py:180
  73.6 0.0 all-to-all-done
  73.6 0.4 turn.1
  74.0 0.0 copy-start
  74.0 1.0 copy-done
  75.0 9.6 %all-to-all-start.1 = ((bf16[16,280,128]{2,1,0:T(8,128)(2,1)}), bf16[16,280,128]{2,1,0:T(8,128)(2,1)S(1)}, u32[]{:S(2)}, u32[]{:S(2)}) async-start(bf16[16,280,128]{2,1,0:T(8,128)(2,1)} %copy-done), calls=%async_computation.1 | async-start | bytes 2293760 | tf_op jit(solution)/shard_map/all_to_all | solution.py:220
  84.6 0.1 pad_add_fusion.spot_ref
  84.7 0.0 collective-permute-done.5.refs_3_
  84.7 18.9 %collective-permute-done.4.refs_2_ = bf16[4,160,1024]{2,1,0:T(8,128)(2,1)} collective-permute-done((bf16[4,160,1024]{2,1,0:T(8,128)(2,1)}, bf16[4,160,1024]{2,1,0:T(8,128)(2,1)}, u32[]{:S(2)}, u32[]{:S(2)}) %collective-permute-start.4) | collective-permute-done | bytes 1310752 | tf_op jit(solution)/shard_map/ppermute | solution.py:180
  103.6 0.7 all-to-all-done.1.moved_ref
  104.3 4.2 %product.1 = bf16[224,1024]{1,0:T(8,128)(2,1)S(1)} custom-call(s32[3]{0:T(128)S(1)} %pad_add_fusion.spot_ref, bf16[16,280,128]{2,1,0:T(8,128)(2,1)S(1)} %all-to-all-done.1.moved_ref, bf16[4,160,1024]{2,1,0:T(8,128)(2,1)S(1)} %order.1.refs_0_, bf16[4,160,1024]{2,1,0:T(8,128)(2,1)} %collective-permute-done.3.refs_1_, ...), custom_call_target="tpu_custom_call" | custom-call | tf_op jit(solution)/shard_map/product/pallas_call | solution.py:159
  108.5 13.8 %collective-permute-start.7 = (bf16[56,1024]{1,0:T(8,128)(2,1)S(1)}, bf16[56,1024]{1,0:T(8,128)(2,1)S(1)}, u32[]{:S(2)}, u32[]{:S(2)}) collective-permute-start(bf16[56,1024]{1,0:T(8,128)(2,1)S(1)} %get-tuple-element.6), channel_id=1, source_target_pairs={{0,1},{1,2},{2,3},{3,0},{64,67},{65,64},{66,65},{67,66},{128,129},... | collective-permute-start | bytes 344072 | tf_op jit(solution)/shard_map/ppermute | solution.py:180
  122.3 1.9 %collective-permute-start.6 = (bf16[56,1024]{1,0:T(8,128)(2,1)S(1)}, bf16[56,1024]{1,0:T(8,128)(2,1)S(1)}, u32[]{:S(2)}, u32[]{:S(2)}) collective-permute-start(bf16[56,1024]{1,0:T(8,128)(2,1)S(1)} %get-tuple-element.5), channel_id=1, source_target_pairs={{0,3},{1,0},{2,1},{3,2},{64,65},{65,66},{66,67},{67,64},{128,131},... | collective-permute-start | bytes 344072 | tf_op jit(solution)/shard_map/ppermute | solution.py:180
  124.3 2.0 %collective-permute-done.7 = bf16[56,1024]{1,0:T(8,128)(2,1)S(1)} collective-permute-done((bf16[56,1024]{1,0:T(8,128)(2,1)S(1)}, bf16[56,1024]{1,0:T(8,128)(2,1)S(1)}, u32[]{:S(2)}, u32[]{:S(2)}) %collective-permute-start.7) | collective-permute-done | bytes 114720 | tf_op jit(solution)/shard_map/ppermute | solution.py:180
  126.3 13.3 %collective-permute-start.8 = (bf16[56,1024]{1,0:T(8,128)(2,1)S(1)}, bf16[56,1024]{1,0:T(8,128)(2,1)S(1)}, u32[]{:S(2)}, u32[]{:S(2)}) collective-permute-start(bf16[56,1024]{1,0:T(8,128)(2,1)S(1)} %fusion), channel_id=1, source_target_pairs={{0,1},{1,2},{2,3},{3,0},{64,67},{65,64},{66,65},{67,66},{128,129},... | collective-permute-start | bytes 344072 | tf_op jit(solution)/shard_map/ppermute | solution.py:180
  139.6 4.0 %collective-permute-done.6 = bf16[56,1024]{1,0:T(8,128)(2,1)S(1)} collective-permute-done((bf16[56,1024]{1,0:T(8,128)(2,1)S(1)}, bf16[56,1024]{1,0:T(8,128)(2,1)S(1)}, u32[]{:S(2)}, u32[]{:S(2)}) %collective-permute-start.6) | collective-permute-done | bytes 114720 | tf_op jit(solution)/shard_map/ppermute | solution.py:180
  143.6 9.3 %collective-permute-done.8 = bf16[56,1024]{1,0:T(8,128)(2,1)S(1)} collective-permute-done((bf16[56,1024]{1,0:T(8,128)(2,1)S(1)}, bf16[56,1024]{1,0:T(8,128)(2,1)S(1)}, u32[]{:S(2)}, u32[]{:S(2)}) %collective-permute-start.8) | collective-permute-done | bytes 114720 | tf_op jit(solution)/shard_map/ppermute | solution.py:180
  152.9 0.2 reshape.30
  153.1 0.1 copy.7
  153.2 0.2 reshape.35
  153.3 21.1 %all_to_all.15 = bf16[16,2,1792]{2,1,0:T(2,128)(2,1)S(1)} all-to-all(bf16[16,2,1792]{2,1,0:T(2,128)(2,1)S(1)} %reshape.35), channel_id=1, replica_groups=mesh['expert'=16,'y'=4,'x'=4,'micro'=4] {'y','x'}, dimensions={0} | all-to-all | bytes 229376 | tf_op jit(solution)/shard_map/all_to_all | solution.py:226
  174.4 0.2 reshape.36
  174.7 0.9 copy.9
  (4 shorter events, 0.2 us)
Async XLA Ops:
  3.0 12.8 %copy-start.1 = (bf16[160,1024]{1,0:T(8,128)(2,1)S(1)}, bf16[160,1024]{1,0:T(8,128)(2,1)}, u32[]{:S(2)}) copy-start(bf16[160,1024]{1,0:T(8,128)(2,1)} %refs_0_.1) | copy-start | bytes 983044
  3.0 70.6 %all-to-all-start = ((bf16[16,8,4480]{2,1,0:T(8,128)(2,1)}), bf16[16,8,4480]{2,1,0:T(8,128)(2,1)S(1)}, u32[]{:S(2)}, u32[]{:S(2)}) async-start(bf16[16,8,4480]{2,1,0:T(8,128)(2,1)} %bitcast.29), calls=%async_computation | async-start | bytes 2293760 | tf_op jit(solution)/shard_map/all_to_all | solution.py:216
  15.8 11.7 %collective-permute-start = (bf16[160,1024]{1,0:T(8,128)(2,1)S(1)}, bf16[160,1024]{1,0:T(8,128)(2,1)S(1)}, u32[]{:S(2)}, u32[]{:S(2)}) collective-permute-start(bf16[160,1024]{1,0:T(8,128)(2,1)S(1)} %copy-done.1), channel_id=1, source_target_pairs={{0,4},{4,8},{8,12},{12,0},{64,76},{68,64},{72,68},{76,72},{128,132... | collective-permute-start | bytes 983048 | tf_op jit(solution)/shard_map/ppermute | solution.py:180
  19.2 10.2 %collective-permute-start.2 = (bf16[160,1024]{1,0:T(8,128)(2,1)S(1)}, bf16[160,1024]{1,0:T(8,128)(2,1)S(1)}, u32[]{:S(2)}, u32[]{:S(2)}) collective-permute-start(bf16[160,1024]{1,0:T(8,128)(2,1)S(1)} %copy-done.1), channel_id=1, source_target_pairs={{0,12},{4,0},{8,4},{12,8},{64,68},{68,72},{72,76},{76,64},{128,140... | collective-permute-start | bytes 983048 | tf_op jit(solution)/shard_map/ppermute | solution.py:180
  27.4 11.9 %collective-permute-start.1 = (bf16[160,1024]{1,0:T(8,128)(2,1)S(1)}, bf16[160,1024]{1,0:T(8,128)(2,1)S(1)}, u32[]{:S(2)}, u32[]{:S(2)}) collective-permute-start(bf16[160,1024]{1,0:T(8,128)(2,1)S(1)} %collective-permute-done.refs_1_), channel_id=1, source_target_pairs={{0,4},{4,8},{8,12},{12,0},{64,76},{68,64},{72,68},{76,72},{128,132... | collective-permute-start | bytes 983048 | tf_op jit(solution)/shard_map/ppermute | solution.py:180
  39.9 31.6 %collective-permute-start.3 = (bf16[4,160,1024]{2,1,0:T(8,128)(2,1)S(1)}, bf16[4,160,1024]{2,1,0:T(8,128)(2,1)}, u32[]{:S(2)}, u32[]{:S(2)}) collective-permute-start(bf16[4,160,1024]{2,1,0:T(8,128)(2,1)S(1)} %order.1.refs_0_), channel_id=1, source_target_pairs={{0,16},{16,32},{32,48},{48,0},{64,112},{80,64},{96,80},{112,96},{1... | collective-permute-start | bytes 3932168 | tf_op jit(solution)/shard_map/ppermute | solution.py:180
  41.8 42.9 %collective-permute-start.5 = (bf16[4,160,1024]{2,1,0:T(8,128)(2,1)S(1)}, bf16[4,160,1024]{2,1,0:T(8,128)(2,1)}, u32[]{:S(2)}, u32[]{:S(2)}) collective-permute-start(bf16[4,160,1024]{2,1,0:T(8,128)(2,1)S(1)} %order.1.refs_0_), channel_id=1, source_target_pairs={{0,48},{16,0},{32,16},{48,32},{64,80},{80,96},{96,112},{112,64},{1... | collective-permute-start | bytes 3932168 | tf_op jit(solution)/shard_map/ppermute | solution.py:180
  71.4 32.2 %collective-permute-start.4 = (bf16[4,160,1024]{2,1,0:T(8,128)(2,1)}, bf16[4,160,1024]{2,1,0:T(8,128)(2,1)}, u32[]{:S(2)}, u32[]{:S(2)}) collective-permute-start(bf16[4,160,1024]{2,1,0:T(8,128)(2,1)} %collective-permute-done.3.refs_1_), channel_id=1, source_target_pairs={{0,16},{16,32},{32,48},{48,0},{64,112},{80,64},{96,80},{112,96},{1... | collective-permute-start | bytes 3932168 | tf_op jit(solution)/shard_map/ppermute | solution.py:180
  74.0 1.0 copy-start
  75.0 29.3 %all-to-all-start.1 = ((bf16[16,280,128]{2,1,0:T(8,128)(2,1)}), bf16[16,280,128]{2,1,0:T(8,128)(2,1)S(1)}, u32[]{:S(2)}, u32[]{:S(2)}) async-start(bf16[16,280,128]{2,1,0:T(8,128)(2,1)} %copy-done), calls=%async_computation.1 | async-start | bytes 2293760 | tf_op jit(solution)/shard_map/all_to_all | solution.py:220
  108.5 17.8 %collective-permute-start.7 = (bf16[56,1024]{1,0:T(8,128)(2,1)S(1)}, bf16[56,1024]{1,0:T(8,128)(2,1)S(1)}, u32[]{:S(2)}, u32[]{:S(2)}) collective-permute-start(bf16[56,1024]{1,0:T(8,128)(2,1)S(1)} %get-tuple-element.6), channel_id=1, source_target_pairs={{0,1},{1,2},{2,3},{3,0},{64,67},{65,64},{66,65},{67,66},{128,129},... | collective-permute-start | bytes 344072 | tf_op jit(solution)/shard_map/ppermute | solution.py:180
  122.3 21.2 %collective-permute-start.6 = (bf16[56,1024]{1,0:T(8,128)(2,1)S(1)}, bf16[56,1024]{1,0:T(8,128)(2,1)S(1)}, u32[]{:S(2)}, u32[]{:S(2)}) collective-permute-start(bf16[56,1024]{1,0:T(8,128)(2,1)S(1)} %get-tuple-element.5), channel_id=1, source_target_pairs={{0,3},{1,0},{2,1},{3,2},{64,65},{65,66},{66,67},{67,64},{128,131},... | collective-permute-start | bytes 344072 | tf_op jit(solution)/shard_map/ppermute | solution.py:180
  126.3 26.6 %collective-permute-start.8 = (bf16[56,1024]{1,0:T(8,128)(2,1)S(1)}, bf16[56,1024]{1,0:T(8,128)(2,1)S(1)}, u32[]{:S(2)}, u32[]{:S(2)}) collective-permute-start(bf16[56,1024]{1,0:T(8,128)(2,1)S(1)} %fusion), channel_id=1, source_target_pairs={{0,1},{1,2},{2,3},{3,0},{64,67},{65,64},{66,65},{67,66},{128,129},... | collective-permute-start | bytes 344072 | tf_op jit(solution)/shard_map/ppermute | solution.py:180
